TPU v7x, 256 devices: a whole 4x4x8 slice. The times are simulated.
256 devices in a mesh: tm: 4 (over y), dom: 64 (over z, x, core).
Axes of the slice: x: 4, y: 4, z: 8, core: 2. Of those that a mesh axis runs over, the one named last changes fastest.
Arguments:
- memory: float32 [65536, 256], P('dom'), may hold values from -8 to 8
- last_update: int32 [65536], P('dom'), may hold values from -4096 to -1
- src_row: int32 [4, 16384], P('tm', 'dom'), may hold values from 0 to 1023
- event_time: int32 [4, 16384], P('tm', 'dom'), may hold values from 0 to 4095, as said below
- dst_rows: int32 [4, 32768], P('tm', 'dom'), may hold values from 0 to 1023
- dst_slot: int32 [4, 16384], P('tm', 'dom'), may hold values from 0 to 511
- request_rows: int32 [4, 524288], P('tm', 'dom'), may hold values from 0 to 1023
- neighbour_slot: int32 [4, 10, 16384], P('tm', None, 'dom'), may hold values from 0 to 8191
- neighbour_gap: int32 [4, 10, 16384], P('tm', None, 'dom'), may hold values from 0 to 4095
- freq: float32 [256], replicated, may hold values from 0.0001 to 0.1
- phase: float32 [256], replicated, may hold values from -3.140625 to 3.140625
- w_input: bfloat16 [768, 768], replicated, may hold values from -0.21875 to 0.21875
- b_input: float32 [768], replicated, may hold values from -3 to 3
- w_hidden: bfloat16 [256, 768], replicated, may hold values from -0.375 to 0.375
- b_hidden: float32 [768], replicated, may hold values from -3 to 3
- w_query: bfloat16 [512, 256], replicated, may hold values from -0.65625 to 0.65625
- w_key: bfloat16 [512, 256], replicated, may hold values from -0.65625 to 0.65625
- w_value: bfloat16 [512, 256], replicated, may hold values from -0.25 to 0.25
- w_merge: bfloat16 [512, 256], replicated, may hold values from -0.25 to 0.25
- b_merge: float32 [256], replicated, may hold values from -3 to 3
- w_out: bfloat16 [256, 256], replicated, may hold values from -0.375 to 0.375
- b_out: float32 [256], replicated, may hold values from -3 to 3
Outputs:
- new_memory: float32 [4, 65536, 256], P('tm', 'dom')
- embedding: bfloat16 [4, 16384, 256], P('tm', 'dom')
Inputs may be any that keep to these rules, and one draw needn't show every extreme that they name: `event_time`: the events of batch b have times b * 1024 to (b + 1) * 1024 - 1.
All inputs are finite; a program needn't handle non-finite values.
Results may differ from a plain program's by a relative error of at most 0.02.
Values may be sent and summed in bfloat16 or wider, within the bound.
A program may use at most 128 MiB of HBM per device.

v0:
```python
import functools
import math

import jax
import jax.numpy as jnp
from jax import lax
from jax.experimental import pallas as pl
from jax.experimental.pallas import tpu as pltpu
from jax.sharding import PartitionSpec as P

HEADS = 4
MESH = pl.DeviceIdType.MESH
BF = jnp.bfloat16
F32 = jnp.float32


def cosine(x):
    turns = jnp.floor(x * (0.5 / math.pi) + 0.5)
    h = 0.5 * ((x - turns * 6.28125) - turns * (2 * math.pi - 6.28125))
    q = h * h
    s = h + h * q * (
        -1 / 6 + q * (1 / 120 + q * (-1 / 5040 + q * (1 / 362880 - q * (1 / 39916800))))
    )
    return 1.0 - 2.0 * s * s


def dot(a, b):
    return jnp.dot(a, b, preferred_element_type=F32)


def as_column(row):
    lanes = lax.broadcasted_iota(jnp.int32, (128, 128), 1)
    subs = lax.broadcasted_iota(jnp.int32, (128, 128), 0)
    parts = []
    for i in range(row.shape[0]):
        wide = jnp.broadcast_to(row[i : i + 1, :].astype(F32), (128, 128))
        parts.append(jnp.sum(jnp.where(lanes == subs, wide, 0.0), axis=1, keepdims=True))
    return jnp.concatenate(parts, axis=0)


def as_row(row):
    return jnp.concatenate([row[i : i + 1, :] for i in range(row.shape[0])], axis=1)


def split(x):
    hi = x.astype(BF)
    return hi, (x - hi.astype(F32)).astype(BF)


def chain_kernel(
    periods,
    domains,
    memory,
    stamps_in,
    ints,
    freq,
    phase,
    w_input,
    b_input,
    w_hidden,
    b_hidden,
    out_memory,
    out_rows,
    cur,
    hilo,
    ibuf,
    req,
    reqr,
    gsend,
    grecv,
    ohg,
    ohs,
    oht,
    group,
    timed,
    touched,
    inverse,
    ysend_sem,
    yrecv_sem,
    rsend_sem,
    rrecv_sem,
    gsend_sem,
    grecv_sem,
):
    me_t = lax.axis_index("tm")
    me_d = lax.axis_index("dom")
    nodes, width = memory.shape
    events = ohs.shape[1]
    dcap = 8
    asked = domains * dcap
    er = events // 128

    barrier = pltpu.get_barrier_semaphore()

    def greet(i, carry):
        pl.semaphore_signal(
            barrier,
            inc=1,
            device_id={"dom": lax.rem(me_d + i, domains)},
            device_id_type=MESH,
        )
        return carry

    lax.fori_loop(1, domains, greet, 0)
    for i in range(1, periods):
        pl.semaphore_signal(
            barrier,
            inc=1,
            device_id={"tm": lax.rem(me_t + i, periods)},
            device_id_type=MESH,
        )
    pl.semaphore_wait(barrier, domains - 1 + periods - 1)

    for i in range(1, periods):
        pltpu.make_async_remote_copy(
            src_ref=ints,
            dst_ref=ibuf.at[me_t],
            send_sem=ysend_sem,
            recv_sem=yrecv_sem,
            device_id={"tm": lax.rem(me_t + i, periods)},
            device_id_type=MESH,
        ).start()
    cur[...] = memory[...]
    hi, lo = split(memory[...])
    hilo[:, :width] = hi
    hilo[:, width:] = lo
    others = ibuf.at[pl.ds(0, periods - 1)]
    pltpu.make_async_copy(others, others, yrecv_sem).wait()
    ibuf[me_t] = ints[...]

    req[...] = jnp.sum(ibuf[:, :domains, :], axis=0)[:, None, :]

    def ask(i, carry):
        peer = lax.rem(me_d + i, domains)
        pltpu.make_async_remote_copy(
            src_ref=req.at[peer],
            dst_ref=reqr.at[me_d],
            send_sem=rsend_sem,
            recv_sem=rrecv_sem,
            device_id={"dom": peer},
            device_id_type=MESH,
        ).start()
        return carry

    lax.fori_loop(1, domains, ask, 0)

    stamps = stamps_in[...].astype(F32)

    def prepare(b, stamps):
        source_rows = ibuf[b, pl.ds(domains, er), :]
        source = as_column(source_rows)
        moment = as_column(ibuf[b, pl.ds(domains + er, er), :])
        source_row = as_row(source_rows).astype(F32)
        nodes_lane = lax.broadcasted_iota(jnp.int32, (events, nodes), 1).astype(F32)
        picks = source == nodes_lane
        ohs[b] = jnp.where(picks, 1.0, 0.0).astype(BF)
        before = jnp.sum(jnp.where(picks, stamps, 0.0), axis=1, keepdims=True)
        latest = jnp.max(jnp.where(picks, moment, -1.0), axis=0, keepdims=True)
        same = source == source_row
        same_f = jnp.where(same, 1.0, 0.0)
        group[b] = same_f.astype(BF)
        inverse[b] = jnp.broadcast_to(
            1.0 / jnp.sum(same_f, axis=1, keepdims=True), inverse.shape[1:]
        )
        earlier = lax.broadcasted_iota(jnp.int32, same.shape, 0) < lax.broadcasted_iota(
            jnp.int32, same.shape, 1
        )
        first = jnp.sum(jnp.where(same & earlier, 1.0, 0.0), axis=0, keepdims=True) == 0.0
        nodes_sub = lax.broadcasted_iota(jnp.int32, (nodes, events), 0).astype(F32)
        back = jnp.where((source_row == nodes_sub) & first, 1.0, 0.0)
        oht[b] = back.astype(BF)
        touched[b] = jnp.broadcast_to(jnp.sum(back, axis=1, keepdims=True), touched.shape[1:])
        code = cosine((moment - before) * freq[...] + phase[...]).astype(BF)
        timed[b] = dot(code, w_input[2 * width :, :])
        return jnp.where(latest >= 0.0, latest, stamps)

    stamps = prepare(0, stamps)

    reqr[me_d] = req[me_d]
    rest = reqr.at[pl.ds(0, domains - 1)]
    pltpu.make_async_copy(rest, rest, rrecv_sem).wait()

    def asked_picks(b):
        wide = jnp.broadcast_to(reqr[...], (domains, dcap, 128)).reshape(asked, 128)
        lanes = lax.broadcasted_iota(jnp.int32, (asked, 128), 1)
        subs = lax.broadcasted_iota(jnp.int32, (asked, 128), 0)
        wanted = jnp.sum(
            jnp.where(lanes == b * dcap + subs % dcap, wide.astype(F32), 0.0),
            axis=1,
            keepdims=True,
        )
        lane = lax.broadcasted_iota(jnp.int32, (asked, nodes), 1).astype(F32)
        ohg[b] = jnp.where(wanted == lane, 1.0, 0.0).astype(BF)

    asked_picks(0)

    for b in range(periods):

        @pl.when(me_t == b)
        def _():
            out_rows[...] = hilo[:, :width]

        answer = dot(ohg[b], hilo[:, :width])
        answer = jnp.concatenate(
            [
                answer[:, :128].reshape(domains, dcap, 128),
                answer[:, 128:].reshape(domains, dcap, 128),
            ],
            axis=1,
        ).astype(BF)
        gsend[b] = answer

        def send(i, carry, b=b):
            peer = lax.rem(me_d + i, domains)
            pltpu.make_async_remote_copy(
                src_ref=gsend.at[b, peer],
                dst_ref=grecv.at[b, me_d],
                send_sem=gsend_sem.at[b],
                recv_sem=grecv_sem.at[b],
                device_id={"dom": peer},
                device_id_type=MESH,
            ).start()
            return carry

        lax.fori_loop(1, domains, send, 0)

        if b == 0:
            for later in range(1, periods):
                asked_picks(later)
                stamps = prepare(later, stamps)
        own = dot(ohs[b], hilo[...])
        own_hi = own[:, :width].astype(BF)
        own_f = own[:, :width] + own[:, width:]
        projected = dot(own_hi, w_input[:width, :]) + timed[b]
        hidden = dot(own_hi, w_hidden[...]) + b_hidden[...]
        slot = as_column(ibuf[b, pl.ds(domains + 2 * er, er), :]).astype(jnp.int32)
        place = (slot // dcap) * (2 * dcap) + slot % dcap
        lane = lax.broadcasted_iota(jnp.int32, (events, 2 * asked), 1)
        pick_left = jnp.where(lane == place, 1.0, 0.0).astype(BF)
        pick_right = jnp.where(lane == place + dcap, 1.0, 0.0).astype(BF)

        arrived = grecv.at[b, pl.ds(0, domains - 1)]
        pltpu.make_async_copy(arrived, arrived, grecv_sem.at[b]).wait()
        grecv[b, me_d] = gsend[b, me_d]
        fetched = grecv[b].reshape(2 * asked, 128)
        target = jnp.concatenate(
            [dot(pick_left, fetched), dot(pick_right, fetched)], axis=1
        ).astype(BF)
        projected = projected + dot(target, w_input[width : 2 * width, :])
        p_hi, p_lo = split(projected)
        gates = (dot(group[b], p_hi) + dot(group[b], p_lo)) * inverse[b][:, :1] + b_input[...]
        r = jax.nn.sigmoid(gates[:, :width] + hidden[:, :width])
        z = jax.nn.sigmoid(gates[:, width : 2 * width] + hidden[:, width : 2 * width])
        c = jnp.tanh(gates[:, 2 * width :] + r * hidden[:, 2 * width :])
        fresh = (1.0 - z) * c + z * own_f
        f_hi, f_lo = split(fresh)
        spread = dot(oht[b], jnp.concatenate([f_hi, f_lo], axis=1))
        updated = jnp.where(
            touched[b][:, :1] > 0.0, spread[:, :width] + spread[:, width:], cur[...]
        )

        @pl.when(me_t == b)
        def _():
            out_memory[...] = updated

        if b + 1 < periods:
            cur[...] = updated
            hi, lo = split(updated)
            hilo[:, :width] = hi
            hilo[:, width:] = lo

    pltpu.make_async_copy(others, others, ysend_sem).wait()
    pltpu.make_async_copy(rest, rest, rsend_sem).wait()
    for b in range(periods):
        sent = gsend.at[b, pl.ds(0, domains - 1)]
        pltpu.make_async_copy(sent, sent, gsend_sem.at[b]).wait()


def run_chain(memory, last_update, ints, freq, phase, w_input, b_input, w_hidden, b_hidden):
    periods, domains = lax.axis_size("tm"), lax.axis_size("dom")
    nodes, width = memory.shape
    er = 2
    events = er * 128
    dcap = 8
    asked = domains * dcap
    vmem = pl.BlockSpec(memory_space=pltpu.VMEM)
    return pl.pallas_call(
        functools.partial(chain_kernel, periods, domains),
        out_shape=(
            jax.ShapeDtypeStruct((nodes, width), F32),
            jax.ShapeDtypeStruct((nodes, width), BF),
        ),
        in_specs=[vmem] * 9,
        out_specs=(vmem, vmem),
        scratch_shapes=[
            pltpu.VMEM((nodes, width), F32),
            pltpu.VMEM((nodes, 2 * width), BF),
            pltpu.VMEM((periods,) + ints.shape, jnp.int32),
            pltpu.VMEM((domains, 1, 128), jnp.int32),
            pltpu.VMEM((domains, 1, 128), jnp.int32),
            pltpu.VMEM((periods, domains, 2 * dcap, 128), BF),
            pltpu.VMEM((periods, domains, 2 * dcap, 128), BF),
            pltpu.VMEM((periods, asked, nodes), BF),
            pltpu.VMEM((periods, events, nodes), BF),
            pltpu.VMEM((periods, nodes, events), BF),
            pltpu.VMEM((periods, events, events), BF),
            pltpu.VMEM((periods, events, 3 * width), F32),
            pltpu.VMEM((periods, nodes, 128), F32),
            pltpu.VMEM((periods, events, 128), F32),
            pltpu.SemaphoreType.DMA(()),
            pltpu.SemaphoreType.DMA(()),
            pltpu.SemaphoreType.DMA(()),
            pltpu.SemaphoreType.DMA(()),
            pltpu.SemaphoreType.DMA((periods,)),
            pltpu.SemaphoreType.DMA((periods,)),
        ],
        compiler_params=pltpu.CompilerParams(
            collective_id=0, has_side_effects=True, vmem_limit_bytes=48 * 2**20
        ),
        name="chain",
    )(
        memory,
        last_update[None, :],
        ints,
        freq[None, :],
        phase[None, :],
        w_input,
        b_input[None, :],
        w_hidden,
        b_hidden[None, :],
    )


def pack_integers(src_row, event_time, dst_rows, dst_slot):
    domains = lax.axis_size("dom")
    tile = jnp.tile(dst_rows[0].reshape(domains, 8), (1, 16))
    lanes = lax.broadcasted_iota(jnp.int32, tile.shape, 1)
    asks = jnp.where(lanes // 8 == lax.axis_index("tm"), tile, 0)
    rows = [a[0].reshape(-1, 128) for a in (src_row, event_time, dst_slot)]
    return jnp.concatenate([asks, *rows, jnp.zeros((2, 128), jnp.int32)], axis=0)


def time_code(elapsed, freq, phase):
    return jnp.cos(elapsed.astype(jnp.float32)[..., None] * freq + phase)


def fetch_neighbours(rows_half, wanted):
    domains = lax.axis_size("dom")

    def answer_requests(requested):
        return lax.all_to_all(rows_half[requested], "dom", split_axis=0, concat_axis=0, tiled=True)

    fetched = answer_requests(
        lax.all_to_all(wanted.reshape(domains, -1), "dom", split_axis=0, concat_axis=0, tiled=True)
    )
    return fetched.reshape(-1, rows_half.shape[1])


def attend(
    own_rows, neighbours, gaps, freq, phase, w_query, w_key, w_value, w_merge, b_merge, w_out, b_out
):
    events, feature_width = own_rows.shape
    head_width = feature_width // HEADS
    resting = jnp.broadcast_to(
        time_code(jnp.zeros((1,), jnp.int32), freq, phase).astype(jnp.bfloat16),
        (events, phase.shape[0]),
    )
    queries = jnp.dot(
        jnp.concatenate([own_rows, resting], axis=1), w_query, preferred_element_type=jnp.float32
    ).astype(jnp.bfloat16)
    key_input = jnp.concatenate(
        [neighbours, time_code(gaps, freq, phase).astype(jnp.bfloat16)], axis=2
    )
    flattened = key_input.reshape(-1, key_input.shape[-1])
    key_rows = jnp.dot(flattened, w_key, preferred_element_type=jnp.float32).astype(jnp.bfloat16)
    value_rows = jnp.dot(flattened, w_value, preferred_element_type=jnp.float32).astype(
        jnp.bfloat16
    )
    key_rows = key_rows.reshape(neighbours.shape[0], events, HEADS, head_width)
    value_rows = value_rows.reshape(neighbours.shape[0], events, HEADS, head_width)
    scores = jnp.einsum(
        "ehd,nehd->neh",
        queries.reshape(events, HEADS, head_width),
        key_rows,
        preferred_element_type=jnp.float32,
    ) / math.sqrt(head_width)
    weights = jax.nn.softmax(scores, axis=0).astype(jnp.bfloat16)
    attended = jnp.einsum("neh,nehd->ehd", weights, value_rows, preferred_element_type=jnp.float32)
    attended = attended.reshape(events, feature_width).astype(jnp.bfloat16)
    merged = jax.nn.relu(
        jnp.dot(
            jnp.concatenate([attended, own_rows], axis=1),
            w_merge,
            preferred_element_type=jnp.float32,
        )
        + b_merge
    ).astype(jnp.bfloat16)
    return (jnp.dot(merged, w_out, preferred_element_type=jnp.float32) + b_out).astype(jnp.bfloat16)


def on_device(
    memory,
    last_update,
    src_row,
    event_time,
    dst_rows,
    dst_slot,
    request_rows,
    neighbour_slot,
    neighbour_gap,
    freq,
    phase,
    w_input,
    b_input,
    w_hidden,
    b_hidden,
    w_query,
    w_key,
    w_value,
    w_merge,
    b_merge,
    w_out,
    b_out,
):
    ints = pack_integers(src_row, event_time, dst_rows, dst_slot)
    updated, rows_half = run_chain(
        memory, last_update, ints, freq, phase, w_input, b_input, w_hidden, b_hidden
    )
    fetched_rows = fetch_neighbours(rows_half, request_rows[0])
    neighbours = fetched_rows[neighbour_slot[0]]
    embedded = attend(
        rows_half[src_row[0]],
        neighbours,
        neighbour_gap[0],
        freq,
        phase,
        w_query,
        w_key,
        w_value,
        w_merge,
        b_merge,
        w_out,
        b_out,
    )
    return (updated[None], embedded[None])


def solution(mesh):
    return jax.shard_map(
        on_device,
        mesh=mesh,
        in_specs=(
            P("dom", None),
            P("dom"),
            P("tm", "dom"),
            P("tm", "dom"),
            P("tm", "dom"),
            P("tm", "dom"),
            P("tm", "dom"),
            P("tm", None, "dom"),
            P("tm", None, "dom"),
            P(),
            P(),
            P(),
            P(),
            P(),
            P(),
            P(),
            P(),
            P(),
            P(),
            P(),
            P(),
            P(),
        ),
        out_specs=(P("tm", "dom", None), P("tm", "dom", None)),
        check_vma=False,
    )
```

profile of v0, /device:TPU:1, one launch (start us, length us, event | category | flops | bytes accessed | tf_op | source)
XLA Modules:
  0.0 256.6 jit_solution(9331259457173171175)
XLA Ops:
  0.6 13.1 %all-to-all-start = ((s32[64,1,128]{2,1,0:T(1,128)}), s32[64,1,128]{2,1,0:T(1,128)S(1)}, u32[]{:S(2)}, u32[]{:S(2)}) async-start(s32[64,1,128]{2,1,0:T(1,128)} %bitcast.57), calls=%async_computation | async-start | bytes 65536 | tf_op jit(solution)/shard_map/all_to_all | solution.py:354
  14.3 1.3 reduce.11
  17.3 0.7 concatenate.15.ints
  18.1 1.3 copy-done.1
  19.3 1.2 copy-done.2
  20.5 1.0 copy-done.3
  23.6 68.5 %chain.1 = (f32[1024,256]{1,0:T(8,128)S(1)}, bf16[1024,256]{1,0:T(8,128)(2,1)S(1)}) custom-call(f32[1024,256]{1,0:T(8,128)S(1)} %copy-done.2, s32[1,1024]{1,0:T(1,128)S(1)} %bitcast.53, s32[72,128]{1,0:T(8,128)S(1)} %concatenate.15.ints, f32[1,256]{1,0:T(1,128)S(1)} %bitcast.51, f32[1,256]{1,0:T(1,128)S(1)} %bitcast.52, bf16[768,768]{1,0:T(8,128)(2,1)S(1)} %copy-done.1, ...), custom_call_target="tpu_custom_call" | custom-call | tf_op jit(solution)/shard_map/chain/pallas_call | solution.py:287
  92.1 33.1 %gather_fusion = bf16[8192,256]{1,0:T(8,128)(2,1)} fusion(bf16[1024,256]{1,0:T(8,128)(2,1)S(1)} %get-tuple-element.5, s32[8192]{0:T(1024)S(1)} %fusion.16), kind=kCustom, calls=%fused_computation | custom fusion | bytes 8421376 | tf_op jit(solution)/shard_map/gather | solution.py:351
  125.2 8.1 %all-to-all-start.1 = ((bf16[64,128,256]{2,1,0:T(8,128)(2,1)}), bf16[64,128,256]{2,1,0:T(8,128)(2,1)}, u32[]{:S(2)}, u32[]{:S(2)}) async-start(bf16[64,128,256]{2,1,0:T(8,128)(2,1)} %bitcast.54), calls=%async_computation.1 | async-start | bytes 8388608 | tf_op jit(solution)/shard_map/all_to_all | solution.py:351
  133.5 1.2 gather_fusion.2
  134.8 1.0 bitcast_convert_fusion.1
  135.8 10.3 %cosine_convert_fusion = bf16[2560,256]{1,0:T(8,128)(2,1)} fusion(f32[256]{0:T(256)S(1)} %copy-done.7, f32[256]{0:T(256)S(1)} %copy-done.5, f32[2560]{0:T(1024)S(1)} %convert_element_type.43), kind=kLoop, calls=%fused_computation.8 | loop fusion | flops 1966080 | bytes 1323008 | tf_op jit(solution)/shard_map/convert_element_type | solution.py:372
  146.0 81.7 %all-to-all-done.1 = bf16[64,128,256]{2,1,0:T(8,128)(2,1)} async-done(((bf16[64,128,256]{2,1,0:T(8,128)(2,1)}), bf16[64,128,256]{2,1,0:T(8,128)(2,1)}, u32[]{:S(2)}, u32[]{:S(2)}) %all-to-all-start.1) | async-done | bytes 4194336 | tf_op jit(solution)/shard_map/all_to_all | solution.py:351
  227.7 9.6 %gather_fusion.1 = bf16[2560,256]{1,0:T(8,128)(2,1)} fusion(bf16[8192,256]{1,0:T(8,128)(2,1)} %bitcast.15, s32[3072]{0:T(1024)S(1)} %pad_clamp_fusion), kind=kCustom, calls=%fused_computation.1 | custom fusion | bytes 2631680 | tf_op jit(solution)/shard_map/gather | solution.py:430
  237.3 2.6 convolution_convert_fusion.1
  239.9 1.6 copy.36
  241.5 2.6 %reshape.132 = bf16[10,256,4,64]{1,0,3,2:T(8,128)(2,1)S(1)} reshape(bf16[2560,256]{0,1:T(8,128)(2,1)} %copy.36) | data formatting | bytes 2621440 | tf_op jit(solution)/shard_map/reshape | solution.py:379
  244.1 1.6 multiply_reduce_fusion.1
  246.5 0.8 convolution_convert_fusion
  247.4 1.6 copy.37
  248.9 2.6 %reshape.134 = bf16[10,256,4,64]{1,0,3,2:T(8,128)(2,1)S(1)} reshape(bf16[2560,256]{0,1:T(8,128)(2,1)} %copy.37) | data formatting | bytes 2621440 | tf_op jit(solution)/shard_map/reshape | solution.py:380
  251.6 1.8 multiply_reduce_fusion
  253.5 2.1 fusion.3
  255.6 1.0 copy.63
  (63 shorter events, 5.3 us)
Async XLA Ops:
  0.6 236.7 %copy-start = (bf16[512,256]{1,0:T(8,128)(2,1)S(1)}, bf16[512,256]{1,0:T(8,128)(2,1)}, u32[]{:S(2)}) copy-start(bf16[512,256]{1,0:T(8,128)(2,1)} %param.38) | copy-start | bytes 786436
  0.6 91.4 %all-to-all-start = ((s32[64,1,128]{2,1,0:T(1,128)}), s32[64,1,128]{2,1,0:T(1,128)S(1)}, u32[]{:S(2)}, u32[]{:S(2)}) async-start(s32[64,1,128]{2,1,0:T(1,128)} %bitcast.57), calls=%async_computation | async-start | bytes 65536 | tf_op jit(solution)/shard_map/all_to_all | solution.py:354
  18.1 1.3 copy-start.1
  19.3 1.2 copy-start.2
  20.5 1.0 copy-start.3
  21.5 0.7 copy-start.4
  22.2 0.7 copy-start.6
  22.9 0.7 copy-start.8
  125.2 8.1 %copy-start.13 = (s32[1,10,256]{2,0,1:T(1,128)S(1)}, s32[1,10,256]{2,0,1:T(1,128)}, u32[]{:S(2)}) copy-start(s32[1,10,256]{2,0,1:T(1,128)} %param.29) | copy-start | bytes 30724
  125.2 8.2 %copy-start.14 = (s32[1,10,256]{2,0,1:T(1,128)S(1)}, s32[1,10,256]{2,0,1:T(1,128)}, u32[]{:S(2)}) copy-start(s32[1,10,256]{2,0,1:T(1,128)} %param.30) | copy-start | bytes 30724
  125.2 8.3 %copy-start.15 = (s32[1,256]{1,0:T(1,128)S(1)}, s32[1,256]{1,0:T(1,128)}, u32[]{:S(2)}) copy-start(s32[1,256]{1,0:T(1,128)} %param.24) | copy-start | bytes 3076
  125.2 9.4 %copy-start.5 = (f32[256]{0:T(256)S(1)}, f32[256]{0:T(256)}, u32[]{:S(2)}) copy-start(f32[256]{0:T(256)} %param.31) | copy-start | bytes 3076
  125.2 9.5 %copy-start.7 = (f32[256]{0:T(256)S(1)}, f32[256]{0:T(256)}, u32[]{:S(2)}) copy-start(f32[256]{0:T(256)} %param.32) | copy-start | bytes 3076
  125.2 9.5 %copy-start.12 = (bf16[512,256]{1,0:T(8,128)(2,1)S(1)}, bf16[512,256]{1,0:T(8,128)(2,1)}, u32[]{:S(2)}) copy-start(bf16[512,256]{1,0:T(8,128)(2,1)} %param.37) | copy-start | bytes 786436
  125.2 102.5 %all-to-all-start.1 = ((bf16[64,128,256]{2,1,0:T(8,128)(2,1)}), bf16[64,128,256]{2,1,0:T(8,128)(2,1)}, u32[]{:S(2)}, u32[]{:S(2)}) async-start(bf16[64,128,256]{2,1,0:T(8,128)(2,1)} %bitcast.54), calls=%async_computation.1 | async-start | bytes 8388608 | tf_op jit(solution)/shard_map/all_to_all | solution.py:351
  134.7 93.1 %copy-start.11 = (bf16[256,256]{1,0:T(8,128)(2,1)}, bf16[256,256]{1,0:T(8,128)(2,1)S(1)}, u32[]{:S(2)}) copy-start(bf16[256,256]{1,0:T(8,128)(2,1)S(1)} %gather_fusion.2) | copy-start | bytes 393220
  244.1 2.4 copy-start.9
  244.1 2.4 copy-start.10
  244.1 2.4 copy-start.16
  248.9 4.6 %copy-start.17 = (f32[256]{0:T(256)S(1)}, f32[256]{0:T(256)}, u32[]{:S(2)}) copy-start(f32[256]{0:T(256)} %param.43) | copy-start | bytes 3076
  248.9 4.6 %copy-start.18 = (f32[256]{0:T(256)S(1)}, f32[256]{0:T(256)}, u32[]{:S(2)}) copy-start(f32[256]{0:T(256)} %param.41) | copy-start | bytes 3076
where the time goes:
time: 258 us; the launch traced here: 257 us
  waiting for transfers between devices  81.7 us (32%)
  Pallas kernels  68.5 us (27%)
  local copies, waits for them, and re-layouts  62.4 us (24%)
  starting transfers between devices  21.2 us (8%)
  other arithmetic  15.4 us (6%)
  matrix products  6.48 us (3%)
    all_to_all x1, waiting for transfers between devices, answer_requests(): lax.all_to_all(rows_half[requested], 'dom', split_axis=0, concat_axis=0,...  81.7 us
    pallas_call x1, Pallas kernels, run_chain(): pl.pallas_call(functools.partial(chain_kernel, periods, domains), out_sha...  68.5 us
    gather x1, local copies, waits for them, and re-layouts, answer_requests(): rows_half[requested]  33.1 us
    all_to_all x1, starting transfers between devices, fetch_neighbours(): lax.all_to_all(wanted.reshape(domains, -1), 'dom', split_axis=0, concat_a...  13.1 us
    convert_element_type x1, other arithmetic, attend(): time_code(gaps, freq, phase).astype(jnp.bfloat16)  10.3 us
    gather x1, local copies, waits for them, and re-layouts, on_device(): neighbours = fetched_rows[neighbour_slot[0]]  9.55 us
    all_to_all x1, starting transfers between devices, answer_requests(): lax.all_to_all(rows_half[requested], 'dom', split_axis=0, concat_axis=0,...  8.08 us
    unnamed x41, local copies, waits for them, and re-layouts  7.72 us
  transfers between devices with their start and end apart: 2, of which 1 were waited for; matrix products, arithmetic and copies ran while one was open for 7% of the time, Pallas kernels for 27%

commit v1 on v0

--- a/solution.py
+++ b/solution.py
@@ -9,6 +9,7 @@
 from jax.sharding import PartitionSpec as P
 
 HEADS = 4
+GROUP = 8
 MESH = pl.DeviceIdType.MESH
 BF = jnp.bfloat16
 F32 = jnp.float32
@@ -340,62 +341,305 @@
     return jnp.concatenate([asks, *rows, jnp.zeros((2, 128), jnp.int32)], axis=0)
 
 
-def time_code(elapsed, freq, phase):
-    return jnp.cos(elapsed.astype(jnp.float32)[..., None] * freq + phase)
-
-
-def fetch_neighbours(rows_half, wanted):
+def near_kernel(
+    domains,
+    rows,
+    asks,
+    slots,
+    gaps,
+    source,
+    freq,
+    phase,
+    w_query,
+    w_key,
+    w_value,
+    w_merge,
+    b_merge,
+    w_out,
+    b_out,
+    out,
+    store,
+    answers,
+    arrived,
+    asked,
+    slot_col,
+    picked,
+    timed,
+    scores,
+    values,
+    query,
+    up_send,
+    up_recv,
+    down_send,
+    down_recv,
+    ask_send,
+    ask_recv,
+    answer_send,
+    answer_recv,
+):
+    nz = domains // GROUP
+    me = lax.axis_index("dom")
+    my_z, my_j = me // GROUP, me % GROUP
+    above = lax.rem(me + GROUP, domains)
+    below = lax.rem(me + domains - GROUP, domains)
+    nodes, width = rows.shape
+    half = nodes // 2
+    neighbours, events = slots.shape
+    offsets = [0]
+    for step in range(1, nz // 2):
+        offsets += [step, -step]
+    offsets += [nz // 2]
+
+    def mate(i):
+        return my_z * GROUP + lax.rem(my_j + i, GROUP)
+
+    barrier = pltpu.get_barrier_semaphore()
+    for peer in [above, below] + [mate(i) for i in range(1, GROUP)]:
+        pl.semaphore_signal(barrier, inc=1, device_id={"dom": peer}, device_id_type=MESH)
+    pl.semaphore_wait(barrier, GROUP + 1)
+
+    def pass_on(step, part, up):
+        origin = lax.rem(my_z + (nz - step if up else step), nz)
+        span = pl.ds(part * half, half)
+        src = rows.at[span] if step == 0 else store.at[origin, span]
+        send, recv = (up_send, up_recv) if up else (down_send, down_recv)
+        return pltpu.make_async_remote_copy(
+            src_ref=src,
+            dst_ref=store.at[origin, span],
+            send_sem=send.at[step, part],
+            recv_sem=recv.at[step, part],
+            device_id={"dom": above if up else below},
+            device_id_type=MESH,
+        )
+
+    def take(step, part, up):
+        origin = lax.rem(my_z + (nz - step - 1 if up else step + 1), nz)
+        here = store.at[origin, pl.ds(part * half, half)]
+        recv = up_recv if up else down_recv
+        pltpu.make_async_copy(here, here, recv.at[step, part]).wait()
+
+    last = nz // 2 - 1
+
+    def moves(step, part, up):
+        return step < last or part == (0 if up else 1)
+
+    for part in range(2):
+        for up in (True, False):
+            if moves(0, part, up):
+                pass_on(0, part, up).start()
+
+    for i in range(1, GROUP):
+        peer_j = lax.rem(my_j + i, GROUP)
+        pltpu.make_async_remote_copy(
+            src_ref=asks.at[:, peer_j],
+            dst_ref=asked.at[my_j],
+            send_sem=ask_send,
+            recv_sem=ask_recv,
+            device_id={"dom": mate(i)},
+            device_id_type=MESH,
+        ).start()
+    asked[my_j] = asks[:, my_j]
+
+    src_col = as_column(source[...])
+    lane = lax.broadcasted_iota(jnp.int32, (events, nodes), 1).astype(F32)
+    own = dot(jnp.where(src_col == lane, 1.0, 0.0).astype(BF), rows[...]).astype(BF)
+    still = jnp.broadcast_to(cosine(phase[...]).astype(BF), (events, width))
+    query[...] = (dot(own, w_query[:width, :]) + dot(still, w_query[width:, :])).astype(BF)
+
+    def prepare(k, carry):
+        here = pl.ds(k * events, events)
+        gap = gaps[pl.ds(k, 1), :]
+        slot = slots[pl.ds(k, 1), :]
+        both = [
+            jnp.concatenate(
+                [as_column(v[:, j * 128 : (j + 1) * 128]) for j in range(events // 128)], axis=0
+            )
+            for v in (gap, slot)
+        ]
+        code = cosine(both[0] * freq[...] + phase[...]).astype(BF)
+        timed[here, :width] = dot(code, w_key[width:, :])
+        timed[here, width:] = dot(code, w_value[width:, :])
+        slot_col[here, :] = jnp.broadcast_to(both[1], (events, 128))
+        return carry
+
+    rest = asked.at[pl.ds(0, GROUP - 1)]
+    pltpu.make_async_copy(rest, rest, ask_recv).wait()
+
+    def answer(i):
+        offset = offsets[i]
+        origin = lax.rem(my_z + offset + nz, nz)
+        if offset:
+            step = abs(offset) - 1
+            for part in range(2):
+                if step < last:
+                    ups = [offset < 0]
+                else:
+                    ups = [part == 0]
+                for up in ups:
+                    take(step, part, up)
+                    if step < last and moves(step + 1, part, up):
+                        pass_on(step + 1, part, up).start()
+        lane = lax.broadcasted_iota(jnp.int32, (GROUP // 2 * 128, nodes), 1).astype(F32)
+        for side in range(2):
+            wanted = jnp.concatenate(
+                [
+                    as_column(asked[side * (GROUP // 2) + j, origin])
+                    for j in range(GROUP // 2)
+                ],
+                axis=0,
+            )
+            pick = jnp.where(wanted == lane, 1.0, 0.0).astype(BF)
+            block = rows[...] if offset == 0 else store[origin]
+            found = dot(pick, block).astype(BF)
+            answers[i, pl.ds(side * (GROUP // 2), GROUP // 2)] = found.reshape(
+                GROUP // 2, 128, width
+            )
+        for j in range(1, GROUP):
+            pltpu.make_async_remote_copy(
+                src_ref=answers.at[i, lax.rem(my_j + j, GROUP)],
+                dst_ref=arrived.at[i, my_j],
+                send_sem=answer_send.at[i],
+                recv_sem=answer_recv.at[i],
+                device_id={"dom": mate(j)},
+                device_id_type=MESH,
+            ).start()
+
+    def select(i):
+        origin = lax.rem(my_z + offsets[i] + nz, nz)
+        here = arrived.at[i, pl.ds(0, GROUP - 1)]
+        pltpu.make_async_copy(here, here, answer_recv.at[i]).wait()
+        arrived[i, my_j] = answers[i, my_j]
+        block = arrived[i].reshape(GROUP * 128, width)
+        base = origin * (GROUP * 128)
+
+        def some(k, carry):
+            here = pl.ds(k * 2 * events, 2 * events)
+            lane = (
+                lax.broadcasted_iota(jnp.int32, (2 * events, GROUP * 128), 1) + base
+            ).astype(F32)
+            wide = slot_col[here, :1]
+            part = dot(jnp.where(wide == lane, 1.0, 0.0).astype(BF), block)
+            if i == 0:
+                picked[here, :] = part
+            else:
+                picked[here, :] = picked[here, :] + part
+            return carry
+
+        lax.fori_loop(0, neighbours // 2, some, 0)
+
+    answer(0)
+    lax.fori_loop(0, neighbours, prepare, 0)
+    for i in range(1, nz):
+        answer(i)
+        select(i - 1)
+    select(nz - 1)
+
+    head = width // HEADS
+    same_head = (
+        lax.broadcasted_iota(jnp.int32, (width, width), 0) // head
+        == lax.broadcasted_iota(jnp.int32, (width, width), 1) // head
+    )
+    heads = jnp.where(same_head, 1.0, 0.0).astype(BF)
+    query_f = query[...].astype(F32)
+    query_2 = jnp.concatenate([query_f, query_f], axis=0)
+
+    def score(k, carry):
+        here = pl.ds(k * 2 * events, 2 * events)
+        near = picked[here, :].astype(BF)
+        key = (dot(near, w_key[:width, :]) + timed[here, :width]).astype(BF)
+        values[here, :] = (dot(near, w_value[:width, :]) + timed[here, width:]).astype(BF)
+        hi, lo = split(query_2 * key.astype(F32))
+        scores[here, :] = (dot(hi, heads) + dot(lo, heads)) * (1.0 / math.sqrt(head))
+        return carry
+
+    lax.fori_loop(0, neighbours // 2, score, 0)
+
+    def slab(ref, k):
+        return ref[k * events : (k + 1) * events, :]
+
+    top = slab(scores, 0)
+    for k in range(1, neighbours):
+        top = jnp.maximum(top, slab(scores, k))
+    total = jnp.zeros_like(top)
+    for k in range(neighbours):
+        raised = jnp.exp(slab(scores, k) - top)
+        scores[k * events : (k + 1) * events, :] = raised
+        total = total + raised
+    scale = 1.0 / total
+    attended = jnp.zeros_like(top)
+    for k in range(neighbours):
+        weight = (slab(scores, k) * scale).astype(BF).astype(F32)
+        attended = attended + weight * slab(values, k).astype(F32)
+    merged = dot(attended.astype(BF), w_merge[:width, :]) + dot(own, w_merge[width:, :])
+    merged = jnp.maximum(merged + b_merge[...], 0.0).astype(BF)
+    out[...] = (dot(merged, w_out[...]) + b_out[...]).astype(BF)
+
+    for step in range(nz // 2):
+        for part in range(2):
+            for up in (True, False):
+                if moves(step, part, up):
+                    pass_on(step, part, up).wait_send()
+    pltpu.make_async_copy(rest, rest, ask_send).wait()
+    for i in range(nz):
+        sent = answers.at[i, pl.ds(0, GROUP - 1)]
+        pltpu.make_async_copy(sent, sent, answer_send.at[i]).wait()
+
+
+def run_near(
+    rows, request_rows, slots, gaps, source, freq, phase,
+    w_query, w_key, w_value, w_merge, b_merge, w_out, b_out,
+):
     domains = lax.axis_size("dom")
-
-    def answer_requests(requested):
-        return lax.all_to_all(rows_half[requested], "dom", split_axis=0, concat_axis=0, tiled=True)
-
-    fetched = answer_requests(
-        lax.all_to_all(wanted.reshape(domains, -1), "dom", split_axis=0, concat_axis=0, tiled=True)
+    nz = domains // GROUP
+    nodes, width = rows.shape
+    neighbours, events = slots.shape
+    pairs = neighbours * events
+    vmem = pl.BlockSpec(memory_space=pltpu.VMEM)
+    return pl.pallas_call(
+        functools.partial(near_kernel, domains),
+        out_shape=jax.ShapeDtypeStruct((events, width), BF),
+        in_specs=[vmem] * 14,
+        out_specs=vmem,
+        scratch_shapes=[
+            pltpu.VMEM((nz, nodes, width), BF),
+            pltpu.VMEM((nz, GROUP, 128, width), BF),
+            pltpu.VMEM((nz, GROUP, 128, width), BF),
+            pltpu.VMEM((GROUP, nz, 1, 128), jnp.int32),
+            pltpu.VMEM((pairs, 128), F32),
+            pltpu.VMEM((pairs, width), F32),
+            pltpu.VMEM((pairs, 2 * width), F32),
+            pltpu.VMEM((pairs, width), F32),
+            pltpu.VMEM((pairs, width), BF),
+            pltpu.VMEM((events, width), BF),
+            pltpu.SemaphoreType.DMA((nz // 2, 2)),
+            pltpu.SemaphoreType.DMA((nz // 2, 2)),
+            pltpu.SemaphoreType.DMA((nz // 2, 2)),
+            pltpu.SemaphoreType.DMA((nz // 2, 2)),
+            pltpu.SemaphoreType.DMA(()),
+            pltpu.SemaphoreType.DMA(()),
+            pltpu.SemaphoreType.DMA((nz,)),
+            pltpu.SemaphoreType.DMA((nz,)),
+        ],
+        compiler_params=pltpu.CompilerParams(
+            collective_id=1, has_side_effects=True, vmem_limit_bytes=48 * 2**20
+        ),
+        name="near",
+    )(
+        rows,
+        request_rows.reshape(nz, GROUP, 1, 128),
+        slots,
+        gaps,
+        source.reshape(-1, 128),
+        freq[None, :],
+        phase[None, :],
+        w_query,
+        w_key,
+        w_value,
+        w_merge,
+        b_merge[None, :],
+        w_out,
+        b_out[None, :],
     )
-    return fetched.reshape(-1, rows_half.shape[1])
-
-
-def attend(
-    own_rows, neighbours, gaps, freq, phase, w_query, w_key, w_value, w_merge, b_merge, w_out, b_out
-):
-    events, feature_width = own_rows.shape
-    head_width = feature_width // HEADS
-    resting = jnp.broadcast_to(
-        time_code(jnp.zeros((1,), jnp.int32), freq, phase).astype(jnp.bfloat16),
-        (events, phase.shape[0]),
-    )
-    queries = jnp.dot(
-        jnp.concatenate([own_rows, resting], axis=1), w_query, preferred_element_type=jnp.float32
-    ).astype(jnp.bfloat16)
-    key_input = jnp.concatenate(
-        [neighbours, time_code(gaps, freq, phase).astype(jnp.bfloat16)], axis=2
-    )
-    flattened = key_input.reshape(-1, key_input.shape[-1])
-    key_rows = jnp.dot(flattened, w_key, preferred_element_type=jnp.float32).astype(jnp.bfloat16)
-    value_rows = jnp.dot(flattened, w_value, preferred_element_type=jnp.float32).astype(
-        jnp.bfloat16
-    )
-    key_rows = key_rows.reshape(neighbours.shape[0], events, HEADS, head_width)
-    value_rows = value_rows.reshape(neighbours.shape[0], events, HEADS, head_width)
-    scores = jnp.einsum(
-        "ehd,nehd->neh",
-        queries.reshape(events, HEADS, head_width),
-        key_rows,
-        preferred_element_type=jnp.float32,
-    ) / math.sqrt(head_width)
-    weights = jax.nn.softmax(scores, axis=0).astype(jnp.bfloat16)
-    attended = jnp.einsum("neh,nehd->ehd", weights, value_rows, preferred_element_type=jnp.float32)
-    attended = attended.reshape(events, feature_width).astype(jnp.bfloat16)
-    merged = jax.nn.relu(
-        jnp.dot(
-            jnp.concatenate([attended, own_rows], axis=1),
-            w_merge,
-            preferred_element_type=jnp.float32,
-        )
-        + b_merge
-    ).astype(jnp.bfloat16)
-    return (jnp.dot(merged, w_out, preferred_element_type=jnp.float32) + b_out).astype(jnp.bfloat16)
 
 
 def on_device(
@@ -426,12 +670,12 @@
     updated, rows_half = run_chain(
         memory, last_update, ints, freq, phase, w_input, b_input, w_hidden, b_hidden
     )
-    fetched_rows = fetch_neighbours(rows_half, request_rows[0])
-    neighbours = fetched_rows[neighbour_slot[0]]
-    embedded = attend(
-        rows_half[src_row[0]],
-        neighbours,
+    embedded = run_near(
+        rows_half,
+        request_rows[0],
+        neighbour_slot[0],
         neighbour_gap[0],
+        src_row[0],
         freq,
         phase,
         w_query,

time: 258 us -> 155 us (0.60)
  waiting for transfers between devices: 81.7 us -> 0 us
  Pallas kernels: 68.5 us -> 143 us
  local copies, waits for them, and re-layouts: 62.4 us -> 10.1 us
  starting transfers between devices: 21.2 us -> 0 us
  other arithmetic: 15.4 us -> 1.39 us
  matrix products: 6.48 us -> 0 us
    all_to_all x2 -> x0, waiting for transfers between devices: 81.7 us -> none  [the longest x1 81.7 us: answer_requests(): lax.all_to_all(rows_half[requested], 'dom', split_axis=0, concat_axis=0,...]
    pallas_call x0 -> x1, Pallas kernels: none -> 70.3 us  [run_near(): pl.pallas_call(functools.partial(near_kernel, domains), out_shape=jax.Sha...]
    gather x3 -> x0, local copies, waits for them, and re-layouts: 43.8 us -> none  [the longest x1 33.1 us: answer_requests(): rows_half[requested]]
    all_to_all x2 -> x0, starting transfers between devices: 21.2 us -> none  [the longest x1 13.1 us: fetch_neighbours(): lax.all_to_all(wanted.reshape(domains, -1), 'dom', split_axis=0, concat_a...]
    convert_element_type x3 -> x0, other arithmetic: 10.3 us -> none  [the longest x1 10.3 us: attend(): time_code(gaps, freq, phase).astype(jnp.bfloat16)]
    dot_general x4 -> x0, matrix products: 6.48 us -> none  [the longest x1 2.55 us: attend(): jnp.dot(flattened, w_key, preferred_element_type=jnp.float32)]
    reshape x2 -> x0, local copies, waits for them, and re-layouts: 5.24 us -> none  [the longest x1 2.63 us: attend(): value_rows.reshape(neighbours.shape[0], events, HEADS, head_width)]
    pallas_call x1, Pallas kernels: 68.5 us -> 72.5 us  [run_chain(): pl.pallas_call(functools.partial(chain_kernel, periods, domains), out_sha...]
  transfers between devices with their start and end apart: 2 -> 0, of which waited for: 1 -> 0; matrix products, arithmetic and copies ran while one was open for 7% -> 0% of each run, Pallas kernels for 27% -> 0%
where the time goes in v1:
time: 155 us
  Pallas kernels  143 us (92%)
  local copies, waits for them, and re-layouts  10.1 us (7%)
    pallas_call x1, Pallas kernels, run_chain(): pl.pallas_call(functools.partial(chain_kernel, periods, domains), out_sha...  72.5 us
    pallas_call x1, Pallas kernels, run_near(): pl.pallas_call(functools.partial(near_kernel, domains), out_shape=jax.Sha...  70.3 us
    unnamed x38, local copies, waits for them, and re-layouts  7.74 us

profile of v1, /device:TPU:1, one launch (start us, length us, event | category | flops | bytes accessed | tf_op | source)
XLA Modules:
  0.0 155.0 jit_solution(3218053849833902032)
XLA Ops:
  0.6 0.5 broadcast.27
  1.2 1.3 reduce.3
  2.5 0.1 tile.10
  2.6 0.1 copy.24
  2.7 0.1 copy.25
  2.8 0.7 concatenate.3.ints
  3.5 0.7 broadcast_in_dim.38.b_input
  4.2 0.7 broadcast_in_dim.39.b_hidden
  4.9 1.3 copy-done
  6.2 1.2 copy-done.1
  7.4 1.0 copy-done.2
  8.4 0.7 copy-done.10
  9.1 0.7 copy-done.11
  9.8 0.7 copy-done.12
  10.5 0.0 copy-start.5
  10.5 0.0 copy-start.6
  10.5 0.0 copy-start.7
  10.5 0.0 copy-start.8
  10.5 0.0 copy-start.13
  10.5 0.0 copy-start.14
  10.5 72.5 %chain.1 = (f32[1024,256]{1,0:T(8,128)S(1)}, bf16[1024,256]{1,0:T(8,128)(2,1)S(1)}) custom-call(f32[1024,256]{1,0:T(8,128)S(1)} %copy-done.1, s32[1,1024]{1,0:T(1,128)S(1)} %bitcast.26, s32[72,128]{1,0:T(8,128)S(1)} %concatenate.3.ints, f32[1,256]{1,0:T(1,128)S(1)} %bitcast.22, f32[1,256]{1,0:T(1,128)S(1)} %bitcast.24, bf16[768,768]{1,0:T(8,128)(2,1)S(1)} %copy-done, ...), custom_call_target="tpu_custom_call" | custom-call | tf_op jit(solution)/shard_map/chain/pallas_call | solution.py:288
  83.1 70.3 %near.1 = bf16[256,256]{1,0:T(8,128)(2,1)S(1)} custom-call(bf16[1024,256]{1,0:T(8,128)(2,1)S(1)} %get-tuple-element.5.rows, s32[8,8,1,128]{3,2,1,0:T(1,128)S(1)} %bitcast.19, s32[10,256]{1,0:T(8,128)S(1)} %get-tuple-element.9.slots, s32[10,256]{1,0:T(8,128)S(1)} %get-tuple-element.8.gaps, s32[2,128]{1,0:T(2,128)S(1)} %bitcast.21, f32[1,256]{1,0:T(1,128)S(1)} %bitcast.23, ...), custom_call_target="tpu_custom_call" | custom-call | tf_op jit(solution)/shard_map/near/pallas_call | solution.py:598
  153.4 1.0 copy.32
  154.4 0.7 copy.33
  (28 shorter events, 0.1 us)
Async XLA Ops:
  4.9 1.3 copy-start
  6.2 1.2 copy-start.1
  7.4 1.0 copy-start.2
  8.4 0.7 copy-start.10
  9.1 0.7 copy-start.11
  9.8 0.7 copy-start.12
  10.4 72.6 %copy-start.15 = (s32[1,10,256]{2,0,1:T(1,128)S(1)}, s32[1,10,256]{2,0,1:T(1,128)}, u32[]{:S(2)}) copy-start(s32[1,10,256]{2,0,1:T(1,128)} %param.30) | copy-start | bytes 30724
  10.4 72.6 %copy-start.16 = (s32[1,10,256]{2,0,1:T(1,128)S(1)}, s32[1,10,256]{2,0,1:T(1,128)}, u32[]{:S(2)}) copy-start(s32[1,10,256]{2,0,1:T(1,128)} %param.29) | copy-start | bytes 30724
  10.5 72.6 %copy-start.3 = (bf16[512,256]{1,0:T(8,128)(2,1)S(1)}, bf16[512,256]{1,0:T(8,128)(2,1)}, u32[]{:S(2)}) copy-start(bf16[512,256]{1,0:T(8,128)(2,1)} %w_query.1) | copy-start | bytes 786436
  10.5 72.6 %copy-start.4 = (bf16[512,256]{1,0:T(8,128)(2,1)S(1)}, bf16[512,256]{1,0:T(8,128)(2,1)}, u32[]{:S(2)}) copy-start(bf16[512,256]{1,0:T(8,128)(2,1)} %w_key.1) | copy-start | bytes 786436
  10.5 72.6 %copy-start.5 = (bf16[512,256]{1,0:T(8,128)(2,1)S(1)}, bf16[512,256]{1,0:T(8,128)(2,1)}, u32[]{:S(2)}) copy-start(bf16[512,256]{1,0:T(8,128)(2,1)} %w_value.1) | copy-start | bytes 786436
  10.5 72.6 %copy-start.6 = (bf16[512,256]{1,0:T(8,128)(2,1)S(1)}, bf16[512,256]{1,0:T(8,128)(2,1)}, u32[]{:S(2)}) copy-start(bf16[512,256]{1,0:T(8,128)(2,1)} %w_merge.1) | copy-start | bytes 786436
  10.5 72.6 %copy-start.7 = (bf16[256,256]{1,0:T(8,128)(2,1)S(1)}, bf16[256,256]{1,0:T(8,128)(2,1)}, u32[]{:S(2)}) copy-start(bf16[256,256]{1,0:T(8,128)(2,1)} %w_out.1) | copy-start | bytes 393220
  10.5 72.6 %copy-start.8 = (s32[1,8192]{1,0:T(1,128)S(1)}, s32[1,8192]{1,0:T(1,128)}, u32[]{:S(2)}) copy-start(s32[1,8192]{1,0:T(1,128)} %param.28) | copy-start | bytes 98308
  10.5 72.6 %copy-start.9 = (s32[1,256]{1,0:T(1,128)S(1)}, s32[1,256]{1,0:T(1,128)}, u32[]{:S(2)}) copy-start(s32[1,256]{1,0:T(1,128)} %param.24) | copy-start | bytes 3076
  10.5 72.6 %copy-start.13 = (f32[256]{0:T(256)S(1)}, f32[256]{0:T(256)}, u32[]{:S(2)}) copy-start(f32[256]{0:T(256)} %param.41) | copy-start | bytes 3076
  10.5 72.6 %copy-start.14 = (f32[256]{0:T(256)S(1)}, f32[256]{0:T(256)}, u32[]{:S(2)}) copy-start(f32[256]{0:T(256)} %param.43) | copy-start | bytes 3076

commit v2 on v0

v2 whole, which is shorter than its diff:
```python
import functools
import math

import jax
import jax.numpy as jnp
from jax import lax
from jax.experimental import pallas as pl
from jax.experimental.pallas import tpu as pltpu
from jax.sharding import PartitionSpec as P

HEADS = 4
GROUP = 8
DCAP = 8
CAP = 128
HALVES = 2
MESH = pl.DeviceIdType.MESH
BF = jnp.bfloat16
F32 = jnp.float32


def cosine(x):
    turns = jnp.floor(x * (0.5 / math.pi) + 0.5)
    h = 0.5 * ((x - turns * 6.28125) - turns * (2 * math.pi - 6.28125))
    q = h * h
    s = h + h * q * (
        -1 / 6 + q * (1 / 120 + q * (-1 / 5040 + q * (1 / 362880 - q * (1 / 39916800))))
    )
    return 1.0 - 2.0 * s * s


def dot(a, b):
    return jnp.dot(a, b, preferred_element_type=F32)


def as_column(row):
    lanes = lax.broadcasted_iota(jnp.int32, (128, 128), 1)
    subs = lax.broadcasted_iota(jnp.int32, (128, 128), 0)
    parts = []
    for i in range(row.shape[0]):
        wide = jnp.broadcast_to(row[i : i + 1, :].astype(F32), (128, 128))
        parts.append(jnp.sum(jnp.where(lanes == subs, wide, 0.0), axis=1, keepdims=True))
    return jnp.concatenate(parts, axis=0)


def as_row(row):
    return jnp.concatenate([row[i : i + 1, :] for i in range(row.shape[0])], axis=1)


def split(x):
    hi = x.astype(BF)
    return hi, (x - hi.astype(F32)).astype(BF)


def two_level(column):
    rest = jnp.floor(column * (1 / 128))
    lanes = lax.broadcasted_iota(jnp.int32, (column.shape[0], 128), 1).astype(F32)
    ones = jnp.where(column - rest * 128 == lanes, 1.0, 0.0).astype(BF)
    return ones, jnp.broadcast_to(rest, ones.shape).astype(BF)


def picks_of(ones, rest, first, count):
    none = jnp.zeros_like(ones)
    return jnp.concatenate(
        [jnp.where(rest == first + jnp.bfloat16(t), ones, none) for t in range(count)], axis=1
    )


def start_copy(src, dst, send_sem, recv_sem, device_id):
    copy = pltpu.make_async_remote_copy(
        src_ref=src,
        dst_ref=dst,
        send_sem=send_sem,
        recv_sem=recv_sem,
        device_id=device_id,
        device_id_type=MESH,
    )
    copy.start()


def wait_bytes(ref, sem):
    pltpu.make_async_copy(ref, ref, sem).wait()


def whole_kernel(periods, domains, *refs):
    inputs, (out_memory, out), scratch = refs[:22], refs[22:24], refs[24:]
    staged = scratch[:22]
    (
        cur,
        stamps_in,
        src_in,
        time_in,
        dst_in,
        dslot_in,
        asks,
        slots,
        gaps,
        freq_in,
        phase_in,
        w_input,
        b_input_in,
        w_hidden,
        b_hidden_in,
        w_query,
        w_key,
        w_value,
        w_merge,
        b_merge_in,
        w_out,
        b_out_in,
    ) = staged
    (
        hilo,
        ints,
        ibuf,
        req,
        reqr,
        gsend,
        grecv,
        ohg,
        ohs,
        oht,
        group,
        timed,
        touched,
        inverse,
        rows,
        store,
        answers,
        arrived,
        asked,
        ask_ones,
        ask_rest,
        slot_ones,
        slot_rest,
        picked,
        near_timed,
        scores,
        values,
        in_sem,
        ysend_sem,
        yrecv_sem,
        rsend_sem,
        rrecv_sem,
        gsend_sem,
        grecv_sem,
        up_send,
        up_recv,
        down_send,
        down_recv,
        ask_send,
        ask_recv,
        answer_send,
        answer_recv,
    ) = scratch[22:]

    me_t = lax.axis_index("tm")
    me = lax.axis_index("dom")
    nz = domains // GROUP
    my_z, my_j = me // GROUP, me % GROUP
    nodes, width = cur.shape
    half = nodes // 2
    neighbours, events = slots.shape
    er = events // 128
    asked_rows = domains * DCAP

    def fetch(i):
        return pltpu.make_async_copy(inputs[i], staged[i], in_sem.at[i])

    order = [4, 2, 3, 5, 6] + [0, 1] + list(range(7, 22))
    for i in order:
        fetch(i).start()

    barrier = pltpu.get_barrier_semaphore()

    def greet(i, carry):
        pl.semaphore_signal(
            barrier,
            inc=1,
            device_id={"dom": lax.rem(me + i, domains)},
            device_id_type=MESH,
        )
        return carry

    lax.fori_loop(1, domains, greet, 0)
    for i in range(1, periods):
        pl.semaphore_signal(
            barrier,
            inc=1,
            device_id={"tm": lax.rem(me_t + i, periods)},
            device_id_type=MESH,
        )
    for i in order[:5]:
        fetch(i).wait()
    row = 0
    ints[...] = jnp.zeros_like(ints)
    for ref in (dst_in, src_in, time_in, dslot_in):
        for j in range(ref.shape[1] // 128):
            ints[row : row + 1, :] = ref[:, j * 128 : (j + 1) * 128]
            row += 1
    ar = dst_in.shape[1] // 128
    pl.semaphore_wait(barrier, domains - 1 + periods - 1)

    for i in range(1, periods):
        start_copy(
            ints, ibuf.at[me_t], ysend_sem, yrecv_sem, {"tm": lax.rem(me_t + i, periods)}
        )

    mates = [(1, 0), (3, 0), (1, 1), (3, 1), (2, 0), (2, 1), (0, 1)]
    if GROUP == 2:
        mates = [(0, 1)]

    def mate(dx, dc):
        return ((my_j // 2 + dx) % (GROUP // 2)) * 2 + (my_j + dc) % 2

    for dx, dc in mates:
        peer = mate(dx, dc)
        start_copy(
            asks.at[:, peer], asked.at[my_j], ask_send, ask_recv, {"dom": my_z * GROUP + peer}
        )
    asked[my_j] = asks[:, my_j]
    for i in order[5:]:
        fetch(i).wait()
    hi, lo = split(cur[...])
    hilo[:, :width] = hi
    hilo[:, width:] = lo
    freq = freq_in[...].reshape(1, -1)
    phase = phase_in[...].reshape(1, -1)
    b_input = b_input_in[...].reshape(1, -1)
    b_hidden = b_hidden_in[...].reshape(1, -1)
    ibuf[me_t] = ints[...]
    others = ibuf.at[pl.ds(0, periods - 1)]
    wait_bytes(others, yrecv_sem)

    lanes = lax.broadcasted_iota(jnp.int32, (domains, 128), 1)
    subs = lax.broadcasted_iota(jnp.int32, (domains, 128), 0)
    mine = lanes // DCAP == subs % (128 // DCAP)
    tile = jnp.zeros((domains, 128), F32)
    fold_from = lax.broadcasted_iota(jnp.int32, (128, 128), 0)
    fold_to = lax.broadcasted_iota(jnp.int32, (128, 128), 1)
    for b in range(periods):
        wide = jnp.concatenate(
            [
                jnp.broadcast_to(ibuf[b, j : j + 1, :], (min(16, domains), 128))
                for j in range(max(ar, 1))
            ],
            axis=0,
        )
        kept = jnp.where(mine, wide, 0).astype(F32)
        top = jnp.floor(kept * (1 / 32))
        fold = jnp.where(
            (fold_to // DCAP == b) & (fold_from % DCAP == fold_to % DCAP), 1.0, 0.0
        ).astype(BF)
        tile = tile + 32.0 * dot(top.astype(BF), fold) + dot((kept - 32.0 * top).astype(BF), fold)
    req[...] = tile.astype(jnp.int32)[:, None, :]

    def peer_of(t):
        q, j = t % nz, t // nz
        odd = q % 2
        dz = odd * ((q + 1) // 2) + (1 - odd) * ((nz - q // 2) % nz)
        return ((my_z + dz) % nz) * GROUP + (my_j + j) % GROUP

    def ask(t, carry):
        peer = peer_of(t)
        start_copy(req.at[peer], reqr.at[me], rsend_sem, rrecv_sem, {"dom": peer})
        return carry

    lax.fori_loop(1, domains, ask, 0)
    reqr[me] = req[me]

    def prepare(b, stamps):
        at = b % 2
        source_rows = ibuf[b, pl.ds(ar, er), :]
        source = as_column(source_rows)
        moment = as_column(ibuf[b, pl.ds(ar + er, er), :])
        source_row = as_row(source_rows).astype(F32)
        nodes_lane = lax.broadcasted_iota(jnp.int32, (events, nodes), 1).astype(F32)
        picks = source == nodes_lane
        ohs[at] = jnp.where(picks, 1.0, 0.0).astype(BF)
        before = jnp.sum(jnp.where(picks, stamps, 0.0), axis=1, keepdims=True)
        latest = jnp.max(jnp.where(picks, moment, -1.0), axis=0, keepdims=True)
        same = source == source_row
        same_f = jnp.where(same, 1.0, 0.0)
        group[at] = same_f.astype(BF)
        inverse[at] = jnp.broadcast_to(
            1.0 / jnp.sum(same_f, axis=1, keepdims=True), inverse.shape[1:]
        )
        earlier = lax.broadcasted_iota(jnp.int32, same.shape, 0) < lax.broadcasted_iota(
            jnp.int32, same.shape, 1
        )
        first = jnp.sum(jnp.where(same & earlier, 1.0, 0.0), axis=0, keepdims=True) == 0.0
        nodes_sub = lax.broadcasted_iota(jnp.int32, (nodes, events), 0).astype(F32)
        back = jnp.where((source_row == nodes_sub) & first, 1.0, 0.0)
        oht[at] = back.astype(BF)
        touched[at] = jnp.broadcast_to(jnp.sum(back, axis=1, keepdims=True), touched.shape[1:])
        code = cosine((moment - before) * freq + phase).astype(BF)
        timed[at] = dot(code, w_input[2 * width :, :])
        return jnp.where(latest >= 0.0, latest, stamps)

    def asked_picks(b):
        wide = jnp.broadcast_to(reqr[...], (domains, DCAP, 128)).reshape(asked_rows, 128)
        lanes = lax.broadcasted_iota(jnp.int32, (asked_rows, 128), 1)
        subs = lax.broadcasted_iota(jnp.int32, (asked_rows, 128), 0)
        wanted = jnp.sum(
            jnp.where(lanes == b * DCAP + subs % DCAP, wide.astype(F32), 0.0),
            axis=1,
            keepdims=True,
        )
        ones, rest = two_level(wanted)
        ohg[b % 2] = picks_of(ones, rest, jnp.bfloat16(0), nodes // 128)

    def near_prepare(k, carry):
        here = pl.ds(k * events, events)
        gap, slot = [
            jnp.concatenate(
                [
                    as_column(ref[pl.ds(k, 1), :][:, j * 128 : (j + 1) * 128])
                    for j in range(events // 128)
                ],
                axis=0,
            )
            for ref in (gaps, slots)
        ]
        code = cosine(gap * freq + phase).astype(BF)
        near_timed[here, :width] = dot(code, w_key[width:, :])
        near_timed[here, width:] = dot(code, w_value[width:, :])
        ones, rest = two_level(slot)
        slot_ones[here, :] = ones
        slot_rest[here, :] = rest
        return carry

    def ask_prepare(z, carry):
        for j in range(GROUP):
            ones, rest = two_level(as_column(asked[j, z]))
            ask_ones[z, j * CAP : (j + 1) * CAP, :] = ones
            ask_rest[z, j * CAP : (j + 1) * CAP, :] = rest
        return carry

    def give(b):
        answer = dot(ohg[b % 2], hilo[:, :width])
        gsend[b] = jnp.concatenate(
            [
                answer[:, :128].reshape(domains, DCAP, 128),
                answer[:, 128:].reshape(domains, DCAP, 128),
            ],
            axis=1,
        ).astype(BF)

        def send(t, carry):
            peer = peer_of(t)
            start_copy(
                gsend.at[b, peer],
                grecv.at[b, me],
                gsend_sem.at[b],
                grecv_sem.at[b],
                {"dom": peer},
            )
            return carry

        lax.fori_loop(1, domains, send, 0)
        grecv[b, me] = gsend[b, me]

    def own_share(b):
        own = dot(ohs[b % 2], hilo[...])
        own_hi = own[:, :width].astype(BF)
        own_f = own[:, :width] + own[:, width:]
        projected = dot(own_hi, w_input[:width, :]) + timed[b % 2]
        hidden = dot(own_hi, w_hidden[...]) + b_hidden
        slot = as_column(ibuf[b, pl.ds(ar + 2 * er, er), :]).astype(jnp.int32)
        place = (slot // DCAP) * (2 * DCAP) + slot % DCAP
        lane = lax.broadcasted_iota(jnp.int32, (events, 2 * asked_rows), 1)
        pick_left = jnp.where(lane == place, 1.0, 0.0).astype(BF)
        pick_right = jnp.where(lane == place + DCAP, 1.0, 0.0).astype(BF)
        return own_f, projected, hidden, pick_left, pick_right

    def update(b, share):
        own_f, projected, hidden, pick_left, pick_right = share
        wait_bytes(grecv.at[b, pl.ds(0, domains - 1)], grecv_sem.at[b])
        fetched = grecv[b].reshape(2 * asked_rows, 128)
        target = jnp.concatenate(
            [dot(pick_left, fetched), dot(pick_right, fetched)], axis=1
        ).astype(BF)
        projected = projected + dot(target, w_input[width : 2 * width, :])
        p_hi, p_lo = split(projected)
        at = b % 2
        gates = (dot(group[at], p_hi) + dot(group[at], p_lo)) * inverse[at][:, :1] + b_input
        r = jax.nn.sigmoid(gates[:, :width] + hidden[:, :width])
        z = jax.nn.sigmoid(gates[:, width : 2 * width] + hidden[:, width : 2 * width])
        c = jnp.tanh(gates[:, 2 * width :] + r * hidden[:, 2 * width :])
        fresh = (1.0 - z) * c + z * own_f
        f_hi, f_lo = split(fresh)
        spread = dot(oht[at], jnp.concatenate([f_hi, f_lo], axis=1))
        updated = jnp.where(
            touched[at][:, :1] > 0.0, spread[:, :width] + spread[:, width:], cur[...]
        )

        @pl.when(me_t == b)
        def _():
            out_memory[...] = updated

        if b + 1 < periods:
            cur[...] = updated
            hilo[:, :width] = updated.astype(BF)

    stamps = prepare(0, stamps_in[...].reshape(1, -1).astype(F32))
    wait_bytes(reqr.at[pl.ds(0, domains - 1)], rrecv_sem)
    asked_picks(0)

    def spans(count, parts):
        edges = [count * i // parts for i in range(parts + 1)]
        return list(zip(edges[:-1], edges[1:]))

    beside_near = spans(neighbours, periods - 1)
    beside_asks = spans(nz, periods - 1)
    for b in range(periods - 1):
        give(b)
        if b:
            hilo[:, width:] = (cur[...] - hilo[:, :width].astype(F32)).astype(BF)

        @pl.when(me_t == b)
        def _():
            rows[...] = hilo[:, :width]

        share = own_share(b)
        asked_picks(b + 1)
        stamps = prepare(b + 1, stamps)
        lax.fori_loop(*beside_near[b], near_prepare, 0)
        if b == 0:
            wait_bytes(asked.at[pl.ds(0, GROUP - 1)], ask_recv)
        lax.fori_loop(*beside_asks[b], ask_prepare, 0)
        update(b, share)

    @pl.when(me_t == periods - 1)
    def _():
        rows[...] = hilo[:, :width]

    offsets = [0]
    for step in range(1, nz // 2):
        offsets += [step, -step]
    offsets += [nz // 2]
    above = lax.rem(me + GROUP, domains)
    below = lax.rem(me + domains - GROUP, domains)
    last = nz // 2 - 1

    def pass_on(step, part, up):
        origin = lax.rem(my_z + (nz - step if up else step), nz)
        span = pl.ds(part * half, half)
        src = rows.at[span] if step == 0 else store.at[origin, span]
        send, recv = (up_send, up_recv) if up else (down_send, down_recv)
        return pltpu.make_async_remote_copy(
            src_ref=src,
            dst_ref=store.at[origin, span],
            send_sem=send.at[step, part],
            recv_sem=recv.at[step, part],
            device_id={"dom": above if up else below},
            device_id_type=MESH,
        )

    def take(step, part, up):
        origin = lax.rem(my_z + (nz - step - 1 if up else step + 1), nz)
        recv = up_recv if up else down_recv
        wait_bytes(store.at[origin, pl.ds(part * half, half)], recv.at[step, part])

    def moves(step, part, up):
        return step < last or part == (0 if up else 1)

    def answer(i):
        offset = offsets[i]
        origin = lax.rem(my_z + offset + nz, nz)
        if offset:
            step = abs(offset) - 1
            for part in range(2):
                up = offset < 0 if step < last else part == 0
                take(step, part, up)
                if step < last and moves(step + 1, part, up):
                    pass_on(step + 1, part, up).start()
        block = rows if offset == 0 else store.at[origin]
        size = GROUP * CAP // HALVES
        for side in range(HALVES):
            here = pl.ds(side * size, size)
            pick = picks_of(
                ask_ones[origin, here, :],
                ask_rest[origin, here, :],
                jnp.bfloat16(0),
                nodes // 128,
            )
            found = dot(pick, block[...]).astype(BF)
            answers[i, pl.ds(side * (GROUP // HALVES), GROUP // HALVES)] = found.reshape(
                GROUP // HALVES, CAP, width
            )
        for dx, dc in mates:
            peer = mate(dx, dc)
            start_copy(
                answers.at[i, peer],
                arrived.at[i, my_j],
                answer_send.at[i],
                answer_recv.at[i],
                {"dom": my_z * GROUP + peer},
            )
        arrived[i, my_j] = answers[i, my_j]

    def select(i):
        origin = lax.rem(my_z + offsets[i] + nz, nz)
        wait_bytes(arrived.at[i, pl.ds(0, GROUP - 1)], answer_recv.at[i])
        first = jnp.full((1, 128), origin * GROUP, jnp.int32).astype(F32).astype(BF)

        def some(k, carry):
            here = pl.ds(k * 2 * events, 2 * events)
            pick = picks_of(slot_ones[here, :], slot_rest[here, :], first, GROUP)
            part = dot(pick, arrived[i].reshape(GROUP * CAP, width)).astype(BF)
            if i == 0:
                picked[here, :] = part
            else:
                picked[here, :] = picked[here, :] + part
            return carry

        lax.fori_loop(0, neighbours // 2, some, 0)

    for part in range(2):
        for up in (True, False):
            if moves(0, part, up):
                pass_on(0, part, up).start()
    answer(0)
    final = periods - 1
    give(final)
    hilo[:, width:] = (cur[...] - hilo[:, :width].astype(F32)).astype(BF)

    src_col = as_column(ints[pl.ds(ar, er), :])
    lane = lax.broadcasted_iota(jnp.int32, (events, nodes), 1).astype(F32)
    own = dot(jnp.where(src_col == lane, 1.0, 0.0).astype(BF), rows[...]).astype(BF)
    still = jnp.broadcast_to(cosine(phase).astype(BF), (events, width))
    query = (dot(own, w_query[:width, :]) + dot(still, w_query[width:, :])).astype(BF)

    for i in range(1, nz):
        answer(i)
        if i == 2:
            update(final, own_share(final))
        select(i - 1)
    select(nz - 1)

    head = width // HEADS
    same_head = (
        lax.broadcasted_iota(jnp.int32, (width, width), 0) // head
        == lax.broadcasted_iota(jnp.int32, (width, width), 1) // head
    )
    heads = jnp.where(same_head, 1.0, 0.0).astype(BF)
    query_f = query.astype(F32)
    query_2 = jnp.concatenate([query_f, query_f], axis=0)

    def score(k, carry):
        here = pl.ds(k * 2 * events, 2 * events)
        near = picked[here, :]
        key = (dot(near, w_key[:width, :]) + near_timed[here, :width]).astype(BF)
        values[here, :] = (dot(near, w_value[:width, :]) + near_timed[here, width:]).astype(BF)
        hi, lo = split(query_2 * key.astype(F32))
        scores[here, :] = (dot(hi, heads) + dot(lo, heads)) * (1.0 / math.sqrt(head))
        return carry

    lax.fori_loop(0, neighbours // 2, score, 0)

    def slab(ref, k):
        return ref[k * events : (k + 1) * events, :]

    top = slab(scores, 0)
    for k in range(1, neighbours):
        top = jnp.maximum(top, slab(scores, k))
    total = jnp.zeros_like(top)
    for k in range(neighbours):
        raised = jnp.exp(slab(scores, k) - top)
        scores[k * events : (k + 1) * events, :] = raised
        total = total + raised
    scale = 1.0 / total
    attended = jnp.zeros_like(top)
    for k in range(neighbours):
        weight = (slab(scores, k) * scale).astype(BF).astype(F32)
        attended = attended + weight * slab(values, k).astype(F32)
    merged = dot(attended.astype(BF), w_merge[:width, :]) + dot(own, w_merge[width:, :])
    merged = jnp.maximum(merged + b_merge_in[...].reshape(1, -1), 0.0).astype(BF)
    out[...] = (dot(merged, w_out[...]) + b_out_in[...].reshape(1, -1)).astype(BF)

    wait_bytes(others, ysend_sem)
    wait_bytes(reqr.at[pl.ds(0, domains - 1)], rsend_sem)
    for b in range(periods):
        wait_bytes(gsend.at[b, pl.ds(0, domains - 1)], gsend_sem.at[b])
    for step in range(nz // 2):
        for part in range(2):
            for up in (True, False):
                if moves(step, part, up):
                    pass_on(step, part, up).wait_send()
    wait_bytes(asked.at[pl.ds(0, GROUP - 1)], ask_send)
    for i in range(nz):
        wait_bytes(answers.at[i, pl.ds(0, GROUP - 1)], answer_send.at[i])


def on_device(*args):
    periods, domains = lax.axis_size("tm"), lax.axis_size("dom")
    nz = domains // GROUP
    nodes, width = args[0].shape
    neighbours, events = args[7].shape[1:]
    pairs = neighbours * events
    asked = domains * DCAP
    inputs = list(args)
    inputs[6] = args[6].reshape(nz, GROUP, 1, CAP)
    inputs[7] = args[7][0]
    inputs[8] = args[8][0]
    staged = [pltpu.VMEM(a.shape, a.dtype) for a in inputs]
    dma = pltpu.SemaphoreType.DMA
    updated, embedded = pl.pallas_call(
        functools.partial(whole_kernel, periods, domains),
        out_shape=(
            jax.ShapeDtypeStruct((nodes, width), F32),
            jax.ShapeDtypeStruct((events, width), BF),
        ),
        in_specs=[pl.BlockSpec(memory_space=pl.ANY)] * len(inputs),
        out_specs=[pl.BlockSpec(memory_space=pltpu.VMEM)] * 2,
        scratch_shapes=staged
        + [
            pltpu.VMEM((nodes, 2 * width), BF),
            pltpu.VMEM((16, 128), jnp.int32),
            pltpu.VMEM((periods, 16, 128), jnp.int32),
            pltpu.VMEM((domains, 1, 128), jnp.int32),
            pltpu.VMEM((domains, 1, 128), jnp.int32),
            pltpu.VMEM((periods, domains, 2 * DCAP, 128), BF),
            pltpu.VMEM((periods, domains, 2 * DCAP, 128), BF),
            pltpu.VMEM((2, asked, nodes), BF),
            pltpu.VMEM((2, events, nodes), BF),
            pltpu.VMEM((2, nodes, events), BF),
            pltpu.VMEM((2, events, events), BF),
            pltpu.VMEM((2, events, 3 * width), F32),
            pltpu.VMEM((2, nodes, 128), F32),
            pltpu.VMEM((2, events, 128), F32),
            pltpu.VMEM((nodes, width), BF),
            pltpu.VMEM((nz, nodes, width), BF),
            pltpu.VMEM((nz, GROUP, CAP, width), BF),
            pltpu.VMEM((nz, GROUP, CAP, width), BF),
            pltpu.VMEM((GROUP, nz, 1, CAP), jnp.int32),
            pltpu.VMEM((nz, GROUP * CAP, 128), BF),
            pltpu.VMEM((nz, GROUP * CAP, 128), BF),
            pltpu.VMEM((pairs, 128), BF),
            pltpu.VMEM((pairs, 128), BF),
            pltpu.VMEM((pairs, width), BF),
            pltpu.VMEM((pairs, 2 * width), F32),
            pltpu.VMEM((pairs, width), F32),
            pltpu.VMEM((pairs, width), BF),
            dma((len(inputs),)),
            dma(()),
            dma(()),
            dma(()),
            dma(()),
            dma((periods,)),
            dma((periods,)),
            dma((nz // 2, 2)),
            dma((nz // 2, 2)),
            dma((nz // 2, 2)),
            dma((nz // 2, 2)),
            dma(()),
            dma(()),
            dma((nz,)),
            dma((nz,)),
        ],
        compiler_params=pltpu.CompilerParams(
            collective_id=0, has_side_effects=True, vmem_limit_bytes=60 * 2**20
        ),
        name="whole",
    )(*inputs)
    return (updated[None], embedded[None])


def solution(mesh):
    return jax.shard_map(
        on_device,
        mesh=mesh,
        in_specs=(
            P("dom", None),
            P("dom"),
            P("tm", "dom"),
            P("tm", "dom"),
            P("tm", "dom"),
            P("tm", "dom"),
            P("tm", "dom"),
            P("tm", None, "dom"),
            P("tm", None, "dom"),
            P(),
            P(),
            P(),
            P(),
            P(),
            P(),
            P(),
            P(),
            P(),
            P(),
            P(),
            P(),
            P(),
        ),
        out_specs=(P("tm", "dom", None), P("tm", "dom", None)),
        check_vma=False,
    )
```

time: 258 us -> 137 us (0.53)
  waiting for transfers between devices: 81.7 us -> 0 us
  Pallas kernels: 68.5 us -> 132 us
  local copies, waits for them, and re-layouts: 62.4 us -> 4.29 us
  starting transfers between devices: 21.2 us -> 0 us
  other arithmetic: 15.4 us -> 0 us
  matrix products: 6.48 us -> 0 us
    all_to_all x2 -> x0, waiting for transfers between devices: 81.7 us -> none  [the longest x1 81.7 us: answer_requests(): lax.all_to_all(rows_half[requested], 'dom', split_axis=0, concat_axis=0,...]
    pallas_call x1, Pallas kernels: 68.5 us -> 132 us  [on_device(): pl.pallas_call(functools.partial(whole_kernel, periods, domains), out_sha...]
    gather x3 -> x0, local copies, waits for them, and re-layouts: 43.8 us -> none  [the longest x1 33.1 us: answer_requests(): rows_half[requested]]
    all_to_all x2 -> x0, starting transfers between devices: 21.2 us -> none  [the longest x1 13.1 us: fetch_neighbours(): lax.all_to_all(wanted.reshape(domains, -1), 'dom', split_axis=0, concat_a...]
    convert_element_type x3 -> x0, other arithmetic: 10.3 us -> none  [the longest x1 10.3 us: attend(): time_code(gaps, freq, phase).astype(jnp.bfloat16)]
    dot_general x4 -> x0, matrix products: 6.48 us -> none  [the longest x1 2.55 us: attend(): jnp.dot(flattened, w_key, preferred_element_type=jnp.float32)]
    reshape x2 -> x0, local copies, waits for them, and re-layouts: 5.24 us -> none  [the longest x1 2.63 us: attend(): value_rows.reshape(neighbours.shape[0], events, HEADS, head_width)]
    unnamed x41 -> x5, local copies, waits for them, and re-layouts: 7.72 us -> 4.29 us
  transfers between devices with their start and end apart: 2 -> 0, of which waited for: 1 -> 0; matrix products, arithmetic and copies ran while one was open for 7% -> 0% of each run, Pallas kernels for 27% -> 0%
where the time goes in v2:
time: 137 us
  Pallas kernels  132 us (96%)
  local copies, waits for them, and re-layouts  4.29 us (3%)
    pallas_call x1, Pallas kernels, on_device(): pl.pallas_call(functools.partial(whole_kernel, periods, domains), out_sha...  132 us
    unnamed x5, local copies, waits for them, and re-layouts  4.29 us

profile of v2, /device:TPU:1, one launch (start us, length us, event | category | flops | bytes accessed | tf_op | source)
XLA Modules:
  0.0 137.0 jit_solution(16275596971915199759)
XLA Ops:
  0.6 1.3 copy_bitcast_fusion
  2.0 132.0 %whole.1 = (f32[1024,256]{1,0:T(8,128)}, bf16[256,256]{1,0:T(8,128)(2,1)}) custom-call(f32[1024,256]{1,0:T(8,128)} %refs_0_.1, s32[1024]{0:T(1024)} %refs_1_.1, s32[1,256]{1,0:T(1,128)} %refs_2_.1, s32[1,256]{1,0:T(1,128)} %refs_3_.1, s32[1,512]{1,0:T(1,128)} %refs_4_.1, s32[1,256]{1,0:T(1,128)} %refs_5_.1, s32[8,8,1,128]{3,2,1,0:T(1,128)} %bitcast.9, ...), custom_call_target="tpu_custom_call" | custom-call | tf_op jit(solution)/shard_map/whole/pallas_call | solution.py:607
  134.0 0.0 copy-start
  134.0 2.3 %copy.30 = f32[1,1024,256]{2,1,0:T(8,128)} copy(f32[1,1024,256]{2,1,0:T(8,128)} %bitcast.7) | data formatting | bytes 2097152
  136.3 0.0 copy-done
  136.3 0.7 copy.31
Async XLA Ops:
  134.0 2.3 %copy-start = (bf16[256,256]{1,0:T(8,128)(2,1)S(1)}, bf16[256,256]{1,0:T(8,128)(2,1)}, u32[]{:S(2)}) copy-start(bf16[256,256]{1,0:T(8,128)(2,1)} %get-tuple-element.5) | copy-start | bytes 393220

commit v3 on v2

--- a/solution.py
+++ b/solution.py
@@ -13,6 +13,7 @@
 DCAP = 8
 CAP = 128
 HALVES = 2
+LATE = 3
 MESH = pl.DeviceIdType.MESH
 BF = jnp.bfloat16
 F32 = jnp.float32
@@ -91,7 +92,7 @@
         time_in,
         dst_in,
         dslot_in,
-        asks,
+        asks_in,
         slots,
         gaps,
         freq_in,
@@ -109,6 +110,8 @@
         b_out_in,
     ) = staged
     (
+        fresh_memory,
+        asks,
         hilo,
         ints,
         ibuf,
@@ -137,6 +140,7 @@
         scores,
         values,
         in_sem,
+        out_sem,
         ysend_sem,
         yrecv_sem,
         rsend_sem,
@@ -172,16 +176,27 @@
 
     barrier = pltpu.get_barrier_semaphore()
 
-    def greet(i, carry):
+    ways = [nz // 2] + [w for step in range(nz // 2 - 1, 0, -1) for w in (step, nz - step)] + [0]
+    bases = [lax.rem(my_z + way, nz) * GROUP for way in ways]
+
+    def each_peer(visit):
+        for base in bases[:-1]:
+            visit(base + my_j)
+
+        def some(j, carry):
+            place = lax.rem(my_j + j, GROUP)
+            for base in bases:
+                visit(base + place)
+            return carry
+
+        lax.fori_loop(1, GROUP, some, 0)
+
+    def greet(peer):
         pl.semaphore_signal(
-            barrier,
-            inc=1,
-            device_id={"dom": lax.rem(me + i, domains)},
-            device_id_type=MESH,
-        )
-        return carry
-
-    lax.fori_loop(1, domains, greet, 0)
+            barrier, inc=1, device_id={"dom": peer}, device_id_type=MESH
+        )
+
+    each_peer(greet)
     for i in range(1, periods):
         pl.semaphore_signal(
             barrier,
@@ -198,6 +213,10 @@
             ints[row : row + 1, :] = ref[:, j * 128 : (j + 1) * 128]
             row += 1
     ar = dst_in.shape[1] // 128
+    for z in range(nz):
+        for j in range(GROUP):
+            at = (z * GROUP + j) * CAP
+            asks[z, j] = asks_in[:, at : at + CAP]
     pl.semaphore_wait(barrier, domains - 1 + periods - 1)
 
     for i in range(1, periods):
@@ -228,85 +247,6 @@
     b_input = b_input_in[...].reshape(1, -1)
     b_hidden = b_hidden_in[...].reshape(1, -1)
     ibuf[me_t] = ints[...]
-    others = ibuf.at[pl.ds(0, periods - 1)]
-    wait_bytes(others, yrecv_sem)
-
-    lanes = lax.broadcasted_iota(jnp.int32, (domains, 128), 1)
-    subs = lax.broadcasted_iota(jnp.int32, (domains, 128), 0)
-    mine = lanes // DCAP == subs % (128 // DCAP)
-    tile = jnp.zeros((domains, 128), F32)
-    fold_from = lax.broadcasted_iota(jnp.int32, (128, 128), 0)
-    fold_to = lax.broadcasted_iota(jnp.int32, (128, 128), 1)
-    for b in range(periods):
-        wide = jnp.concatenate(
-            [
-                jnp.broadcast_to(ibuf[b, j : j + 1, :], (min(16, domains), 128))
-                for j in range(max(ar, 1))
-            ],
-            axis=0,
-        )
-        kept = jnp.where(mine, wide, 0).astype(F32)
-        top = jnp.floor(kept * (1 / 32))
-        fold = jnp.where(
-            (fold_to // DCAP == b) & (fold_from % DCAP == fold_to % DCAP), 1.0, 0.0
-        ).astype(BF)
-        tile = tile + 32.0 * dot(top.astype(BF), fold) + dot((kept - 32.0 * top).astype(BF), fold)
-    req[...] = tile.astype(jnp.int32)[:, None, :]
-
-    def peer_of(t):
-        q, j = t % nz, t // nz
-        odd = q % 2
-        dz = odd * ((q + 1) // 2) + (1 - odd) * ((nz - q // 2) % nz)
-        return ((my_z + dz) % nz) * GROUP + (my_j + j) % GROUP
-
-    def ask(t, carry):
-        peer = peer_of(t)
-        start_copy(req.at[peer], reqr.at[me], rsend_sem, rrecv_sem, {"dom": peer})
-        return carry
-
-    lax.fori_loop(1, domains, ask, 0)
-    reqr[me] = req[me]
-
-    def prepare(b, stamps):
-        at = b % 2
-        source_rows = ibuf[b, pl.ds(ar, er), :]
-        source = as_column(source_rows)
-        moment = as_column(ibuf[b, pl.ds(ar + er, er), :])
-        source_row = as_row(source_rows).astype(F32)
-        nodes_lane = lax.broadcasted_iota(jnp.int32, (events, nodes), 1).astype(F32)
-        picks = source == nodes_lane
-        ohs[at] = jnp.where(picks, 1.0, 0.0).astype(BF)
-        before = jnp.sum(jnp.where(picks, stamps, 0.0), axis=1, keepdims=True)
-        latest = jnp.max(jnp.where(picks, moment, -1.0), axis=0, keepdims=True)
-        same = source == source_row
-        same_f = jnp.where(same, 1.0, 0.0)
-        group[at] = same_f.astype(BF)
-        inverse[at] = jnp.broadcast_to(
-            1.0 / jnp.sum(same_f, axis=1, keepdims=True), inverse.shape[1:]
-        )
-        earlier = lax.broadcasted_iota(jnp.int32, same.shape, 0) < lax.broadcasted_iota(
-            jnp.int32, same.shape, 1
-        )
-        first = jnp.sum(jnp.where(same & earlier, 1.0, 0.0), axis=0, keepdims=True) == 0.0
-        nodes_sub = lax.broadcasted_iota(jnp.int32, (nodes, events), 0).astype(F32)
-        back = jnp.where((source_row == nodes_sub) & first, 1.0, 0.0)
-        oht[at] = back.astype(BF)
-        touched[at] = jnp.broadcast_to(jnp.sum(back, axis=1, keepdims=True), touched.shape[1:])
-        code = cosine((moment - before) * freq + phase).astype(BF)
-        timed[at] = dot(code, w_input[2 * width :, :])
-        return jnp.where(latest >= 0.0, latest, stamps)
-
-    def asked_picks(b):
-        wide = jnp.broadcast_to(reqr[...], (domains, DCAP, 128)).reshape(asked_rows, 128)
-        lanes = lax.broadcasted_iota(jnp.int32, (asked_rows, 128), 1)
-        subs = lax.broadcasted_iota(jnp.int32, (asked_rows, 128), 0)
-        wanted = jnp.sum(
-            jnp.where(lanes == b * DCAP + subs % DCAP, wide.astype(F32), 0.0),
-            axis=1,
-            keepdims=True,
-        )
-        ones, rest = two_level(wanted)
-        ohg[b % 2] = picks_of(ones, rest, jnp.bfloat16(0), nodes // 128)
 
     def near_prepare(k, carry):
         here = pl.ds(k * events, events)
@@ -328,15 +268,86 @@
         slot_rest[here, :] = rest
         return carry
 
-    def ask_prepare(z, carry):
+    lax.fori_loop(0, 2, near_prepare, 0)
+    others = ibuf.at[pl.ds(0, periods - 1)]
+    wait_bytes(others, yrecv_sem)
+
+    lanes = lax.broadcasted_iota(jnp.int32, (domains, 128), 1)
+    subs = lax.broadcasted_iota(jnp.int32, (domains, 128), 0)
+    mine = lanes // DCAP == subs % (128 // DCAP)
+    tile = jnp.zeros((domains, 128), F32)
+    fold_from = lax.broadcasted_iota(jnp.int32, (128, 128), 0)
+    fold_to = lax.broadcasted_iota(jnp.int32, (128, 128), 1)
+    for b in range(periods):
+        wide = jnp.concatenate(
+            [
+                jnp.broadcast_to(ibuf[b, j : j + 1, :], (min(16, domains), 128))
+                for j in range(max(ar, 1))
+            ],
+            axis=0,
+        )
+        kept = jnp.where(mine, wide, 0).astype(F32)
+        top = jnp.floor(kept * (1 / 32))
+        fold = jnp.where(
+            (fold_to // DCAP == b) & (fold_from % DCAP == fold_to % DCAP), 1.0, 0.0
+        ).astype(BF)
+        tile = tile + 32.0 * dot(top.astype(BF), fold) + dot((kept - 32.0 * top).astype(BF), fold)
+    req[...] = tile.astype(jnp.int32)[:, None, :]
+
+    def ask(peer):
+        start_copy(req.at[peer], reqr.at[me], rsend_sem, rrecv_sem, {"dom": peer})
+
+    each_peer(ask)
+    reqr[me] = req[me]
+
+    def prepare(b, stamps):
+        at = b % 2
+        source_rows = ibuf[b, pl.ds(ar, er), :]
+        source = as_column(source_rows)
+        moment = as_column(ibuf[b, pl.ds(ar + er, er), :])
+        source_row = as_row(source_rows).astype(F32)
+        nodes_lane = lax.broadcasted_iota(jnp.int32, (events, nodes), 1).astype(F32)
+        picks = source == nodes_lane
+        ohs[at] = jnp.where(picks, 1.0, 0.0).astype(BF)
+        before = jnp.sum(jnp.where(picks, stamps, 0.0), axis=1, keepdims=True)
+        latest = jnp.max(jnp.where(picks, moment, -1.0), axis=0, keepdims=True)
+        same = source == source_row
+        same_f = jnp.where(same, 1.0, 0.0)
+        group[at] = same_f.astype(BF)
+        inverse[at] = jnp.broadcast_to(
+            1.0 / jnp.sum(same_f, axis=1, keepdims=True), inverse.shape[1:]
+        )
+        earlier = lax.broadcasted_iota(jnp.int32, same.shape, 0) < lax.broadcasted_iota(
+            jnp.int32, same.shape, 1
+        )
+        first = jnp.sum(jnp.where(same & earlier, 1.0, 0.0), axis=0, keepdims=True) == 0.0
+        nodes_sub = lax.broadcasted_iota(jnp.int32, (nodes, events), 0).astype(F32)
+        back = jnp.where((source_row == nodes_sub) & first, 1.0, 0.0)
+        oht[at] = back.astype(BF)
+        touched[at] = jnp.broadcast_to(jnp.sum(back, axis=1, keepdims=True), touched.shape[1:])
+        code = cosine((moment - before) * freq + phase).astype(BF)
+        timed[at] = dot(code, w_input[2 * width :, :])
+        return jnp.where(latest >= 0.0, latest, stamps)
+
+    def asked_picks(b):
+        wide = jnp.broadcast_to(reqr[...], (domains, DCAP, 128)).reshape(asked_rows, 128)
+        lanes = lax.broadcasted_iota(jnp.int32, (asked_rows, 128), 1)
+        subs = lax.broadcasted_iota(jnp.int32, (asked_rows, 128), 0)
+        wanted = jnp.sum(
+            jnp.where(lanes == b * DCAP + subs % DCAP, wide.astype(F32), 0.0),
+            axis=1,
+            keepdims=True,
+        )
+        ones, rest = two_level(wanted)
+        ohg[b % 2] = picks_of(ones, rest, jnp.bfloat16(0), nodes // 128)
+
+    def ask_prepare(z):
         for j in range(GROUP):
             ones, rest = two_level(as_column(asked[j, z]))
             ask_ones[z, j * CAP : (j + 1) * CAP, :] = ones
             ask_rest[z, j * CAP : (j + 1) * CAP, :] = rest
-        return carry
-
-    def give(b):
-        answer = dot(ohg[b % 2], hilo[:, :width])
+
+    def put_answer(b, answer):
         gsend[b] = jnp.concatenate(
             [
                 answer[:, :128].reshape(domains, DCAP, 128),
@@ -345,8 +356,8 @@
             axis=1,
         ).astype(BF)
 
-        def send(t, carry):
-            peer = peer_of(t)
+    def give(b):
+        def send(peer):
             start_copy(
                 gsend.at[b, peer],
                 grecv.at[b, me],
@@ -354,67 +365,74 @@
                 grecv_sem.at[b],
                 {"dom": peer},
             )
-            return carry
-
-        lax.fori_loop(1, domains, send, 0)
+
+        each_peer(send)
         grecv[b, me] = gsend[b, me]
 
     def own_share(b):
-        own = dot(ohs[b % 2], hilo[...])
+        at = b % 2
+        own = dot(ohs[at], hilo[...])
         own_hi = own[:, :width].astype(BF)
         own_f = own[:, :width] + own[:, width:]
-        projected = dot(own_hi, w_input[:width, :]) + timed[b % 2]
+        p_hi, p_lo = split(dot(own_hi, w_input[:width, :]) + timed[at])
+        base = (dot(group[at], p_hi) + dot(group[at], p_lo)) * inverse[at][:, :1] + b_input
         hidden = dot(own_hi, w_hidden[...]) + b_hidden
         slot = as_column(ibuf[b, pl.ds(ar + 2 * er, er), :]).astype(jnp.int32)
         place = (slot // DCAP) * (2 * DCAP) + slot % DCAP
         lane = lax.broadcasted_iota(jnp.int32, (events, 2 * asked_rows), 1)
-        pick_left = jnp.where(lane == place, 1.0, 0.0).astype(BF)
-        pick_right = jnp.where(lane == place + DCAP, 1.0, 0.0).astype(BF)
-        return own_f, projected, hidden, pick_left, pick_right
+        sums = [
+            dot(group[at], jnp.where(lane == place + j * DCAP, 1.0, 0.0).astype(BF)).astype(BF)
+            for j in range(2)
+        ]
+        return own_f, base, hidden, sums
+
+    def next_share(b):
+        through = dot(ohg[b % 2], oht[(b - 1) % 2])
+        kept = jnp.where(
+            jnp.sum(through, axis=1, keepdims=True) > 0.0, 0.0, dot(ohg[b % 2], hilo[:, :width])
+        )
+        return through.astype(BF), kept
 
     def update(b, share):
-        own_f, projected, hidden, pick_left, pick_right = share
+        own_f, base, hidden, sums = share
         wait_bytes(grecv.at[b, pl.ds(0, domains - 1)], grecv_sem.at[b])
         fetched = grecv[b].reshape(2 * asked_rows, 128)
-        target = jnp.concatenate(
-            [dot(pick_left, fetched), dot(pick_right, fetched)], axis=1
-        ).astype(BF)
-        projected = projected + dot(target, w_input[width : 2 * width, :])
-        p_hi, p_lo = split(projected)
-        at = b % 2
-        gates = (dot(group[at], p_hi) + dot(group[at], p_lo)) * inverse[at][:, :1] + b_input
+        total = jnp.concatenate([dot(sums[0], fetched), dot(sums[1], fetched)], axis=1)
+        m_hi, m_lo = split(total * inverse[b % 2][:, :1])
+        w_target = w_input[width : 2 * width, :]
+        gates = base + dot(m_hi, w_target) + dot(m_lo, w_target)
         r = jax.nn.sigmoid(gates[:, :width] + hidden[:, :width])
         z = jax.nn.sigmoid(gates[:, width : 2 * width] + hidden[:, width : 2 * width])
         c = jnp.tanh(gates[:, 2 * width :] + r * hidden[:, 2 * width :])
-        fresh = (1.0 - z) * c + z * own_f
-        f_hi, f_lo = split(fresh)
-        spread = dot(oht[at], jnp.concatenate([f_hi, f_lo], axis=1))
+        return split((1.0 - z) * c + z * own_f)
+
+    def write_back(b, fresh):
+        at = b % 2
+        spread = dot(oht[at], jnp.concatenate(fresh, axis=1))
         updated = jnp.where(
             touched[at][:, :1] > 0.0, spread[:, :width] + spread[:, width:], cur[...]
         )
 
         @pl.when(me_t == b)
         def _():
-            out_memory[...] = updated
+            fresh_memory[...] = updated
 
         if b + 1 < periods:
             cur[...] = updated
-            hilo[:, :width] = updated.astype(BF)
+            hi, lo = split(updated)
+            hilo[:, :width] = hi
+            hilo[:, width:] = lo
 
     stamps = prepare(0, stamps_in[...].reshape(1, -1).astype(F32))
+    lax.fori_loop(2, 4, near_prepare, 0)
     wait_bytes(reqr.at[pl.ds(0, domains - 1)], rrecv_sem)
     asked_picks(0)
 
-    def spans(count, parts):
-        edges = [count * i // parts for i in range(parts + 1)]
-        return list(zip(edges[:-1], edges[1:]))
-
-    beside_near = spans(neighbours, periods - 1)
-    beside_asks = spans(nz, periods - 1)
+    put_answer(0, dot(ohg[0], hilo[:, :width]))
     for b in range(periods - 1):
         give(b)
         if b:
-            hilo[:, width:] = (cur[...] - hilo[:, :width].astype(F32)).astype(BF)
+            write_back(b - 1, fresh)
 
         @pl.when(me_t == b)
         def _():
@@ -423,11 +441,14 @@
         share = own_share(b)
         asked_picks(b + 1)
         stamps = prepare(b + 1, stamps)
-        lax.fori_loop(*beside_near[b], near_prepare, 0)
+        through, kept = next_share(b + 1)
         if b == 0:
             wait_bytes(asked.at[pl.ds(0, GROUP - 1)], ask_recv)
-        lax.fori_loop(*beside_asks[b], ask_prepare, 0)
-        update(b, share)
+            ask_prepare(my_z)
+        fresh = update(b, share)
+        if b + 2 < periods:
+            put_answer(b + 1, kept + dot(through, fresh[0]))
+    write_back(periods - 2, fresh)
 
     @pl.when(me_t == periods - 1)
     def _():
@@ -521,8 +542,10 @@
                 pass_on(0, part, up).start()
     answer(0)
     final = periods - 1
+    put_answer(final, kept + dot(through, fresh[0]))
     give(final)
-    hilo[:, width:] = (cur[...] - hilo[:, :width].astype(F32)).astype(BF)
+    ask_prepare(lax.rem(my_z + offsets[1] + nz, nz))
+    lax.fori_loop(4, neighbours, near_prepare, 0)
 
     src_col = as_column(ints[pl.ds(ar, er), :])
     lane = lax.broadcasted_iota(jnp.int32, (events, nodes), 1).astype(F32)
@@ -530,11 +553,15 @@
     still = jnp.broadcast_to(cosine(phase).astype(BF), (events, width))
     query = (dot(own, w_query[:width, :]) + dot(still, w_query[width:, :])).astype(BF)
 
+    result = pltpu.make_async_copy(fresh_memory, out_memory, out_sem)
     for i in range(1, nz):
         answer(i)
-        if i == 2:
-            update(final, own_share(final))
+        if i + 1 < nz:
+            ask_prepare(lax.rem(my_z + offsets[i + 1] + nz, nz))
         select(i - 1)
+        if i == LATE:
+            write_back(final, update(final, own_share(final)))
+            result.start()
     select(nz - 1)
 
     head = width // HEADS
@@ -577,6 +604,7 @@
     merged = jnp.maximum(merged + b_merge_in[...].reshape(1, -1), 0.0).astype(BF)
     out[...] = (dot(merged, w_out[...]) + b_out_in[...].reshape(1, -1)).astype(BF)
 
+    result.wait()
     wait_bytes(others, ysend_sem)
     wait_bytes(reqr.at[pl.ds(0, domains - 1)], rsend_sem)
     for b in range(periods):
@@ -599,7 +627,6 @@
     pairs = neighbours * events
     asked = domains * DCAP
     inputs = list(args)
-    inputs[6] = args[6].reshape(nz, GROUP, 1, CAP)
     inputs[7] = args[7][0]
     inputs[8] = args[8][0]
     staged = [pltpu.VMEM(a.shape, a.dtype) for a in inputs]
@@ -611,9 +638,14 @@
             jax.ShapeDtypeStruct((events, width), BF),
         ),
         in_specs=[pl.BlockSpec(memory_space=pl.ANY)] * len(inputs),
-        out_specs=[pl.BlockSpec(memory_space=pltpu.VMEM)] * 2,
+        out_specs=[
+            pl.BlockSpec(memory_space=pl.ANY),
+            pl.BlockSpec(memory_space=pltpu.VMEM),
+        ],
         scratch_shapes=staged
         + [
+            pltpu.VMEM((nodes, width), F32),
+            pltpu.VMEM((nz, GROUP, 1, CAP), jnp.int32),
             pltpu.VMEM((nodes, 2 * width), BF),
             pltpu.VMEM((16, 128), jnp.int32),
             pltpu.VMEM((periods, 16, 128), jnp.int32),
@@ -646,6 +678,7 @@
             dma(()),
             dma(()),
             dma(()),
+            dma(()),
             dma((periods,)),
             dma((periods,)),
             dma((nz // 2, 2)),

time: 137 us -> 132 us (0.964)
  Pallas kernels: 132 us -> 127 us
    pallas_call x1, Pallas kernels: 132 us -> 127 us  [on_device(): pl.pallas_call(functools.partial(whole_kernel, periods, domains), out_sha...]
where the time goes in v3:
time: 132 us
  Pallas kernels  127 us (96%)
  local copies, waits for them, and re-layouts  4.29 us (3%)
    pallas_call x1, Pallas kernels, on_device(): pl.pallas_call(functools.partial(whole_kernel, periods, domains), out_sha...  127 us
    unnamed x5, local copies, waits for them, and re-layouts  4.29 us

profile of v3, /device:TPU:1, one launch (start us, length us, event | category | flops | bytes accessed | tf_op | source)
XLA Modules:
  0.0 131.8 jit_solution(14578595383428311731)
XLA Ops:
  0.6 1.3 %copy_bitcast_fusion = (s32[10,256]{1,0:T(8,128)}, s32[10,256]{1,0:T(8,128)}) fusion(s32[1,10,256]{2,0,1:T(1,128)} %param.30, s32[1,10,256]{2,0,1:T(1,128)} %param.29), kind=kLoop, calls=%fused_computation | loop fusion | bytes 40960
  2.0 126.8 %whole.1 = (f32[1024,256]{1,0:T(8,128)}, bf16[256,256]{1,0:T(8,128)(2,1)}) custom-call(f32[1024,256]{1,0:T(8,128)} %refs_0_.1, s32[1024]{0:T(1024)} %refs_1_.1, s32[1,256]{1,0:T(1,128)} %refs_2_.1, s32[1,256]{1,0:T(1,128)} %refs_3_.1, s32[1,512]{1,0:T(1,128)} %refs_4_.1, s32[1,256]{1,0:T(1,128)} %refs_5_.1, s32[1,8192]{1,0:T(1,128)} %refs_6_.1, ...), custom_call_target="tpu_custom_call" | custom-call | tf_op jit(solution)/shard_map/whole/pallas_call | solution.py:634
  128.8 0.0 copy-start
  128.8 2.3 %copy.30 = f32[1,1024,256]{2,1,0:T(8,128)} copy(f32[1,1024,256]{2,1,0:T(8,128)} %bitcast.6) | data formatting | bytes 2097152
  131.1 0.0 copy-done
  131.1 0.7 copy.31
Async XLA Ops:
  128.8 2.3 %copy-start = (bf16[256,256]{1,0:T(8,128)(2,1)S(1)}, bf16[256,256]{1,0:T(8,128)(2,1)}, u32[]{:S(2)}) copy-start(bf16[256,256]{1,0:T(8,128)(2,1)} %get-tuple-element.5) | copy-start | bytes 393220
